TPU v7x, 32 devices: a whole 2x2x4 slice. The times are simulated.
32 devices in a mesh: noise: 4 (over y, x), row: 8 (over z, core).
Axes of the slice: x: 2, y: 2, z: 4, core: 2. Of those that a mesh axis runs over, the one named last changes fastest.
Arguments:
- activations: bfloat16 [16, 512, 768], P('noise', 'row'), may hold values from -6 to 6
- cond_scale: bfloat16 [16, 512, 768], P('noise', 'row'), may hold values from 0.25 to 16
- cond_shift: bfloat16 [16, 512, 768], P('noise', 'row'), may hold values from -4 to 4
- output_gate: bfloat16 [16, 512, 768], P('noise', 'row'), may hold values from -8 to 8
- pair_repr: bfloat16 [512, 512, 128], P('row', 'noise'), may hold values from -6 to 6
- bias_weight: bfloat16 [128, 8], replicated, may hold values from -1.5 to 1.5
- query_weight: bfloat16 [768, 384], P('noise'), may hold values from -0.21875 to 0.21875
- query_bias: bfloat16 [384], replicated, may hold values from -4 to 4
- key_weight: bfloat16 [768, 384], P('noise'), may hold values from -0.21875 to 0.21875
- value_weight: bfloat16 [768, 384], P('noise'), may hold values from -0.21875 to 0.21875
- output_weight: bfloat16 [384, 768], P('noise'), may hold values from -0.3125 to 0.3125
- token_mask: int32 [16, 512], P('noise', 'row'), may hold values from 0 to 1, as said below
Outputs:
- updated: bfloat16 [16, 512, 768], P('noise', 'row')
Inputs may be any that keep to these rules, and one draw needn't show every extreme that they name: `token_mask`: in each sample the tokens with mask 1 form a prefix of half of 512 tokens or more, and some sample has all 512 tokens.
All inputs are finite; a program needn't handle non-finite values.
Results may differ from a plain program's by a relative error of at most 0.012.
The roundings to bfloat16 on the way count: a program that leaves them out, or rounds other values in their place, can miss the bound.
Values may be sent and summed in bfloat16 or wider, within the bound.
No kernel may reach another device: no remote copies, remote signals or barrier semaphores. Data moves between devices by JAX's collectives and lax.ppermute only.
A program may use at most 128 MiB of HBM per device.

v0:
```python
import functools
import math

import jax
import jax.numpy as jnp
from jax import lax
from jax.experimental import pallas as pl
from jax.experimental.pallas import tpu as pltpu
from jax.sharding import PartitionSpec as P

epsilon = 1e-05
masked_score = -1e30
absent = 32768.0
log2_e = math.log2(math.e)
vmem_bytes = 40 * 2**20
wide_bytes = 60 * 2**20


def layer_norm(tensor):
    average = jnp.mean(tensor, axis=-1, keepdims=True)
    centred = tensor - average
    variance = jnp.mean(centred * centred, axis=-1, keepdims=True)
    return centred * lax.rsqrt(variance + epsilon)


def shift_kernel(
    activations_hbm,
    scale_hbm,
    shift_hbm,
    mask_hbm,
    query_hbm,
    key_hbm,
    shifted,
    sent,
    packed,
    activations,
    cond_scale,
    cond_shift,
    token_mask,
    query_weight,
    key_weight,
    sems,
):
    samples, rows, features = activations.shape
    copies = [pltpu.make_async_copy(mask_hbm, token_mask, sems.at[0])]
    for s in range(samples):
        for t, (source, target) in enumerate(
            ((activations_hbm, activations), (scale_hbm, cond_scale), (shift_hbm, cond_shift))
        ):
            copies.append(pltpu.make_async_copy(source.at[s], target.at[s], sems.at[1 + 3 * s + t]))
    copies.append(pltpu.make_async_copy(query_hbm, query_weight, sems.at[1 + 3 * samples]))
    copies.append(pltpu.make_async_copy(key_hbm, key_weight, sems.at[2 + 3 * samples]))
    for copy in copies:
        copy.start()
    diagonal = lax.broadcasted_iota(jnp.int32, (rows, rows), 0) == lax.broadcasted_iota(
        jnp.int32, (rows, rows), 1
    )
    copies[0].wait()
    for s in range(samples):
        for copy in copies[1 + 3 * s : 4 + 3 * s]:
            copy.wait()
        normed = layer_norm(activations[s].astype(jnp.float32))
        result = cond_scale[s].astype(jnp.float32) * normed + cond_shift[s].astype(jnp.float32)
        flags = jnp.where(diagonal, token_mask[s : s + 1, :].astype(jnp.float32), 0.0)
        valid = jnp.sum(flags, axis=1, keepdims=True) > 0.0
        shifted[s] = result.astype(jnp.bfloat16)
        sent[s] = jnp.where(valid, result, absent).astype(jnp.bfloat16)
    core = lax.rem(lax.axis_index("row"), 2)
    half, breadth = packed.shape[0], query_weight.shape[1]
    for w, weight in enumerate((query_weight, key_weight)):
        copies[1 + 3 * samples + w].wait()
        whole = weight[...].astype(jnp.float32)
        packed[:, w * breadth : (w + 1) * breadth] = jnp.where(
            core == 0, whole[:half], whole[half:]
        ).astype(jnp.bfloat16)


def bias_kernel(pair_hbm, value_hbm, weights, parcel, pair, value_weight, collected, sems):
    pieces, per, columns, channels = pair.shape
    heads = weights.shape[0]
    rows = pieces * per
    copies = [
        pltpu.make_async_copy(pair_hbm.at[pl.ds(i * per, per)], pair.at[i], sems.at[i]) for i in range(pieces)
    ]
    copies.append(pltpu.make_async_copy(value_hbm, value_weight, sems.at[pieces]))
    for copy in copies:
        copy.start()
    twice = jnp.concatenate([weights[...], weights[...]], axis=1)
    for i in range(pieces):
        copies[i].wait()
        normed = layer_norm(pair[i].reshape(per * columns, channels).astype(jnp.float32))
        upper = normed.astype(jnp.bfloat16)
        lower = (normed - upper.astype(jnp.float32)).astype(jnp.bfloat16)
        result = lax.dot_general(
            twice,
            jnp.concatenate([upper, lower], axis=1),
            (((1,), (1,)), ((), ())),
            preferred_element_type=jnp.float32,
        )
        for r in range(per):
            at = (i * per + r) * heads
            collected[at : at + heads, :] = result[:, r * columns : (r + 1) * columns]
    core = lax.rem(lax.axis_index("row"), 2)
    half = columns // 2
    for h in range(heads):
        turned = collected[pl.ds(h, rows, stride=heads), :].T
        low, up = turned[:half], turned[half:]
        both = [jnp.where(core == 0, low, up), jnp.where(core == 0, up, low)]
        parcel[h * half : (h + 1) * half, :] = jnp.concatenate(both, axis=1).astype(jnp.bfloat16)
    copies[pieces].wait()
    depth, breadth = value_weight.shape
    whole = value_weight[...].astype(jnp.float32)
    kept = jnp.where(core == 0, whole[: depth // 2], whole[depth // 2 :]).astype(jnp.bfloat16)
    for t in range(breadth // columns):
        at = heads * half + t * (depth // 2)
        parcel[at : at + depth // 2, :] = kept[:, t * columns : (t + 1) * columns]


def attend_keys(heads, keys, values, penalty, bias_of, queries):
    width = queries.shape[0] // heads
    sums, highs, totals = [], [], []
    for h in range(heads):
        across = slice(h * width, (h + 1) * width)
        score = jnp.dot(keys[:, across], queries[across, :], preferred_element_type=jnp.float32)
        score = score * (log2_e / math.sqrt(width)) + (bias_of(h) * log2_e + penalty)
        high = jnp.max(score, axis=0, keepdims=True)
        probs = jnp.exp2(score - high)
        totals.append(jnp.sum(probs, axis=0, keepdims=True))
        highs.append(high)
        sums.append(
            jnp.dot(values[across, :], probs.astype(jnp.bfloat16), preferred_element_type=jnp.float32)
        )
    return sums, highs, totals


def absent_penalty(tokens):
    return jnp.where(tokens[:, 0:1].astype(jnp.float32) > absent / 2, masked_score, 0.0)


def bias_picker(parcel_mine, parcel_other, steps, first, rows):
    chip = lax.axis_index("row") // 2
    place = lax.axis_index("noise")
    own = lax.broadcasted_iota(jnp.int32, (1, 2 * rows), 1) < rows

    def pick(b, h):
        part = lax.rem(chip - (first + b) + steps, steps) ^ place
        at = slice(h * rows, (h + 1) * rows)
        return jnp.where(own, parcel_mine[part, at].astype(jnp.float32), parcel_other[part, at].astype(jnp.float32))

    return pick


def early_kernel(
    steps, heads, weights_mine, weights_other, query_bias, shifted, shifted_other, parcel_mine, parcel_other, *refs
):
    blocks = refs[: steps - 1]
    partial, queries, key_weight, value_weight, full, full_value = refs[steps - 1 :]
    noise_size, half, _ = weights_mine.shape
    samples, rows, features = shifted.shape
    breadth = key_weight.shape[1]
    width = breadth // heads
    core = lax.rem(lax.axis_index("row"), 2)
    place = lax.axis_index("noise")
    for part, parcel, of_core in (
        (weights_mine, parcel_mine, core),
        (weights_other, parcel_other, 1 - core),
    ):
        for k in range(noise_size):
            start = ((place ^ k) * 2 + of_core) * half
            down = pl.ds(pl.multiple_of(start, math.gcd(half, 32)), half)
            full[down, :] = part[k].astype(full.dtype)
            for t in range(breadth // 128):
                at = heads * rows + t * half
                full_value[down, t * 128 : (t + 1) * 128] = parcel[k, at : at + half].astype(full.dtype)
    key_weight[...] = full[:, breadth : 2 * breadth].astype(jnp.bfloat16)
    value_weight[...] = full_value[...].astype(jnp.float32).T.astype(jnp.bfloat16)
    sides = []
    for tokens in (shifted, shifted_other):
        result = jnp.dot(
            tokens[...].reshape(samples * rows, features),
            full[:, 0:breadth].astype(jnp.bfloat16),
            preferred_element_type=jnp.float32,
        ) + query_bias[...].astype(jnp.float32)
        sides.append(result.astype(jnp.bfloat16).astype(jnp.float32))
    pick = bias_picker(parcel_mine, parcel_other, steps, 0, rows)
    for s in range(samples):
        both = [side[s * rows : (s + 1) * rows] for side in sides]
        queries[s] = jnp.concatenate(both, axis=0).T.astype(jnp.bfloat16)
        tokens = jnp.concatenate([block[s] for block in blocks], axis=0)
        keys = jnp.dot(tokens, key_weight[...], preferred_element_type=jnp.float32).astype(jnp.bfloat16)
        values = lax.dot_general(
            value_weight[...], tokens, (((1,), (1,)), ((), ())), preferred_element_type=jnp.float32
        ).astype(jnp.bfloat16)
        sums, highs, totals = attend_keys(
            heads,
            keys,
            values,
            absent_penalty(tokens),
            lambda h: jnp.concatenate([pick(b, h) for b in range(steps - 1)], axis=0),
            queries.at[s],
        )
        for h in range(heads):
            partial[s, h * width : (h + 1) * width] = sums[h]
            partial[s, breadth + h : breadth + h + 1] = highs[h]
            partial[s, breadth + heads + h : breadth + heads + h + 1] = totals[h]


def late_kernel(
    steps, heads, first, partial, queries, key_weight, value_weight, parcel_mine, parcel_other, block, keep, give, merged
):
    samples = merged.shape[0]
    _, rows, features = block.shape
    breadth = key_weight.shape[1]
    width = breadth // heads
    pick = bias_picker(parcel_mine, parcel_other, steps, steps - 1, rows)
    tokens = block[first : first + samples].reshape(samples * rows, features)
    all_keys = jnp.dot(tokens, key_weight[...], preferred_element_type=jnp.float32).astype(jnp.bfloat16)
    all_values = lax.dot_general(
        value_weight[...], tokens, (((1,), (1,)), ((), ())), preferred_element_type=jnp.float32
    ).astype(jnp.bfloat16)
    penalty = absent_penalty(tokens)
    for s in range(samples):
        here = slice(s * rows, (s + 1) * rows)
        sums, highs, totals = attend_keys(
            heads,
            all_keys[here],
            all_values[:, here],
            penalty[here],
            lambda h: pick(0, h),
            queries.at[first + s],
        )
        before = partial.at[first + s]
        for h in range(heads):
            at_high = slice(breadth + h, breadth + h + 1)
            at_total = slice(breadth + heads + h, breadth + heads + h + 1)
            high = jnp.maximum(before[at_high], highs[h])
            old, new = jnp.exp2(before[at_high] - high), jnp.exp2(highs[h] - high)
            across = slice(h * width, (h + 1) * width)
            merged[s, across] = before[across] * old + sums[h] * new
            merged[s, at_high] = high
            merged[s, at_total] = before[at_total] * old + totals[h] * new
    half = merged.shape[2] // 2
    left = lax.broadcasted_iota(jnp.int32, (1, 2 * half), 1) < half
    for pair in range(samples // 2):
        a, b = merged[2 * pair], merged[2 * pair + 1]
        keep[pair] = jnp.where(left, a, pltpu.roll(b, half, 1))
        give[pair] = jnp.where(left, pltpu.roll(a, half, 1), b)


def finish_kernel(heads, chunks, weight_parts, activations, output_gate, *refs):
    keep, got = refs[:chunks], refs[chunks : 2 * chunks]
    updated, output_weight = refs[2 * chunks :]
    noise_size, part_rows, _ = weight_parts.shape
    breadth = output_weight.shape[0]
    width = breadth // heads
    rows = updated.shape[1]
    place = lax.axis_index("noise")
    for k in range(noise_size):
        down = pl.ds(pl.multiple_of((place ^ k) * part_rows, math.gcd(part_rows, 32)), part_rows)
        output_weight[down, :] = weight_parts[k].astype(output_weight.dtype)
    pairs = keep[0].shape[0]
    for pair in range(chunks * pairs):
        own, other = keep[pair // pairs].at[pair % pairs], got[pair // pairs].at[pair % pairs]
        parts = []
        for h in range(heads):
            at_high = slice(breadth + h, breadth + h + 1)
            at_total = slice(breadth + heads + h, breadth + heads + h + 1)
            across = slice(h * width, (h + 1) * width)
            high = jnp.maximum(own[at_high], other[at_high])
            mine, theirs = jnp.exp2(own[at_high] - high), jnp.exp2(other[at_high] - high)
            total = own[at_total] * mine + other[at_total] * theirs
            parts.append((own[across] * mine + other[across] * theirs) / total)
        attended = jnp.concatenate(parts, axis=0).T.astype(jnp.bfloat16)
        projected = jnp.dot(
            attended, output_weight[...].astype(jnp.bfloat16), preferred_element_type=jnp.float32
        )
        for side in range(2):
            s = 2 * pair + side
            gate = jax.nn.sigmoid(output_gate[s].astype(jnp.float32))
            updated[s] = (
                activations[s].astype(jnp.float32) + gate * projected[side * rows : (side + 1) * rows]
            ).astype(jnp.bfloat16)


def swap_cores(array):
    return lax.ppermute(array, "row", [(i, i ^ 1) for i in range(lax.axis_size("row"))])


def next_chip(array):
    size = lax.axis_size("row")
    return lax.ppermute(array, "row", [(i, (i + 2) % size) for i in range(size)])


def from_noise(array, k):
    if k == 0:
        return array
    return lax.ppermute(array, "noise", [(i, i ^ k) for i in range(lax.axis_size("noise"))])


def body(
    activations,
    cond_scale,
    cond_shift,
    output_gate,
    pair_repr,
    bias_weight,
    query_weight,
    query_bias,
    key_weight,
    value_weight,
    output_weight,
    token_mask,
):
    samples, rows, features = activations.shape
    heads = bias_weight.shape[1]
    head_features = query_weight.shape[1]
    noise_size = lax.axis_size("noise")
    steps = lax.axis_size("row") // 2
    assert noise_size == steps and pair_repr.shape[1] == 2 * rows
    bf16, f32 = jnp.bfloat16, jnp.float32
    params = pltpu.CompilerParams(vmem_limit_bytes=vmem_bytes)
    struct = jax.ShapeDtypeStruct
    after = lax.optimization_barrier
    half = query_weight.shape[0] // 2

    in_hbm = pl.BlockSpec(memory_space=pltpu.HBM)
    shifted, sent, packed = pl.pallas_call(
        shift_kernel,
        in_specs=[in_hbm] * 6,
        out_shape=[struct(activations.shape, bf16)] * 2 + [struct((half, 2 * head_features), bf16)],
        scratch_shapes=[pltpu.VMEM(activations.shape, bf16)] * 3
        + [pltpu.VMEM(token_mask.shape, jnp.int32)]
        + [pltpu.VMEM(query_weight.shape, bf16)] * 2
        + [pltpu.SemaphoreType.DMA((3 * samples + 3,))],
        compiler_params=pltpu.CompilerParams(vmem_limit_bytes=wide_bytes),
        name="shift",
    )(activations, cond_scale, cond_shift, token_mask, query_weight, key_weight)

    ring = [sent, next_chip(sent)]
    weights = [from_noise(packed, k) for k in range(noise_size)]
    shifted_other = swap_cores(shifted)
    pair_repr, _ = after((pair_repr, packed))
    pieces = 8
    columns, channels = pair_repr.shape[1:]
    parcel = pl.pallas_call(
        bias_kernel,
        in_specs=[in_hbm, in_hbm, pl.BlockSpec(memory_space=pltpu.VMEM)],
        out_shape=struct((heads * rows + 3 * half, columns), bf16),
        scratch_shapes=[
            pltpu.VMEM((pieces, rows // pieces, columns, channels), bf16),
            pltpu.VMEM(value_weight.shape, bf16),
            pltpu.VMEM((rows * heads, columns), f32),
            pltpu.SemaphoreType.DMA((pieces + 1,)),
        ],
        compiler_params=pltpu.CompilerParams(vmem_limit_bytes=wide_bytes),
        name="bias",
    )(pair_repr, value_weight, bias_weight.T)

    ring[1], weights, shifted_other, parcel = after((ring[1], weights, shifted_other, parcel))
    ring.append(next_chip(ring[1]))
    weights_mine = jnp.stack(weights)
    weights_other = swap_cores(weights_mine)
    parcels = [from_noise(parcel, k) for k in range(noise_size)]

    ring[2], parcels, weights_other, output_weight = after((ring[2], parcels, weights_other, output_weight))
    for _ in range(steps - 3):
        ring.append(next_chip(ring[-1]))
    last = ring.pop()
    parcel_mine = jnp.stack(parcels)
    parcel_other = swap_cores(parcel_mine)
    output_parts = jnp.stack([from_noise(output_weight, k) for k in range(noise_size)])

    bias_row = query_bias.reshape(1, head_features)
    record = head_features + 2 * heads
    full_type = f32 if half % 16 else bf16
    output_type = f32 if output_weight.shape[0] % 16 else bf16
    partial, queries, key_full, value_full = pl.pallas_call(
        functools.partial(early_kernel, steps, heads),
        out_shape=[
            struct((samples, record, 2 * rows), f32),
            struct((samples, head_features, 2 * rows), bf16),
            struct((features, head_features), bf16),
            struct((head_features, features), bf16),
        ],
        scratch_shapes=[
            pltpu.VMEM((features, 2 * head_features), full_type),
            pltpu.VMEM((features, head_features), full_type),
        ],
        compiler_params=params,
        name="early",
    )(weights_mine, weights_other, bias_row, shifted, shifted_other, parcel_mine, parcel_other, *ring)
    keep, got = [], []
    chunks = 2
    each = samples // chunks
    for c in range(chunks):
        kept, give = pl.pallas_call(
            functools.partial(late_kernel, steps, heads, c * each),
            out_shape=[struct((each // 2, record, 2 * rows), f32)] * 2,
            scratch_shapes=[pltpu.VMEM((each, record, 2 * rows), f32)],
            compiler_params=params,
            name="late",
        )(partial, queries, key_full, value_full, parcel_mine, parcel_other, last)
        keep.append(kept)
        got.append(swap_cores(give))
    return pl.pallas_call(
        functools.partial(finish_kernel, heads, chunks),
        out_shape=struct(activations.shape, bf16),
        scratch_shapes=[pltpu.VMEM((head_features, features), output_type)],
        compiler_params=params,
        name="finish",
    )(output_parts, activations, output_gate, *keep, *got)


def solution(mesh):
    return jax.shard_map(
        body,
        mesh=mesh,
        in_specs=(
            P("noise", "row", None),
            P("noise", "row", None),
            P("noise", "row", None),
            P("noise", "row", None),
            P("row", "noise", None),
            P(),
            P("noise", None),
            P(),
            P("noise", None),
            P("noise", None),
            P("noise", None),
            P("noise", "row"),
        ),
        out_specs=P("noise", "row", None),
        check_vma=False,
    )
```

profile of v0, /device:TPU:0, one launch (start us, length us, event | category | flops | bytes accessed | tf_op | source)
XLA Modules:
  0.0 54.3 jit_solution(14106197645906805175)
XLA Ops:
  0.0 2.9 %shift.1 = (bf16[4,64,768]{2,1,0:T(8,128)(2,1)}, bf16[4,64,768]{2,1,0:T(8,128)(2,1)}, bf16[96,768]{1,0:T(8,128)(2,1)}) custom-call(bf16[4,64,768]{2,1,0:T(8,128)(2,1)} %activations.1, bf16[4,64,768]{2,1,0:T(8,128)(2,1)} %scale_hbm.1, bf16[4,64,768]{2,1,0:T(8,128)(2,1)} %shift_hbm.1, s32[4,64]{1,0:T(4,128)} %mask_hbm.1, bf16[192,384]{1,0:T(8,128)(2,1)} %query_hbm.1, ...), custom_call_target="tpu_custom_call" | custom-call | tf_op jit(solution)/shard_map/shift/pallas_call | solution.py:327
  2.9 0.0 copy-start.5
  2.9 3.1 %collective-permute-start = (bf16[4,64,768]{2,1,0:T(8,128)(2,1)}, bf16[4,64,768]{2,1,0:T(8,128)(2,1)S(1)}, u32[]{:S(2)}, u32[]{:S(2)}) collective-permute-start(bf16[4,64,768]{2,1,0:T(8,128)(2,1)} %get-tuple-element.31.refs_0_), channel_id=1, source_target_pairs={{0,2},{1,3},{2,4},{3,5},{4,6},{5,7},{6,0},{7,1},{8,10},{9,11},{10,... | collective-permute-start | bytes 1179656 | tf_op jit(solution)/shard_map/ppermute | solution.py:291
  6.0 0.0 collective-permute-start.4
  6.0 1.5 %collective-permute-start.1 = (bf16[96,768]{1,0:T(8,128)(2,1)}, bf16[96,768]{1,0:T(8,128)(2,1)S(1)}, u32[]{:S(2)}, u32[]{:S(2)}) collective-permute-start(bf16[96,768]{1,0:T(8,128)(2,1)} %get-tuple-element.37), channel_id=1, source_target_pairs={{0,8},{8,0},{16,24},{24,16},{1,9},{9,1},{17,25},{25,17},{2,10},{10... | collective-permute-start | bytes 442376 | tf_op jit(solution)/shard_map/ppermute | solution.py:297
  7.5 1.5 %collective-permute-start.2 = (bf16[96,768]{1,0:T(8,128)(2,1)}, bf16[96,768]{1,0:T(8,128)(2,1)S(1)}, u32[]{:S(2)}, u32[]{:S(2)}) collective-permute-start(bf16[96,768]{1,0:T(8,128)(2,1)} %get-tuple-element.37), channel_id=1, source_target_pairs={{0,16},{8,24},{16,0},{24,8},{1,17},{9,25},{17,1},{25,9},{2,18},{10... | collective-permute-start | bytes 442376 | tf_op jit(solution)/shard_map/ppermute | solution.py:297
  9.0 0.5 collective-permute-start.3
  9.5 0.0 copy-start.4
  9.5 0.0 copy-start.6
  9.5 0.0 copy-start.2
  9.5 0.0 copy-start.3
  9.5 6.9 %bias.1 = bf16[800,128]{1,0:T(8,128)(2,1)} custom-call(bf16[64,128,128]{2,1,0:T(8,128)(2,1)} %pair_hbm, bf16[192,384]{1,0:T(8,128)(2,1)} %value_hbm.1, bf16[8,128]{1,0:T(8,128)(2,1)} %bitcast.25), custom_call_target="tpu_custom_call" | custom-call | tf_op jit(solution)/shard_map/bias/pallas_call | solution.py:345
  16.5 0.0 collective-permute-done.1
  16.5 0.4 collective-permute-done.2
  16.9 0.0 collective-permute-done.3
  16.9 0.5 collective-permute-done.refs_1_
  17.4 0.0 collective-permute-done.4.shifted_other
  17.4 0.0 copy-done.5
  17.4 0.1 pad_maximum_fusion.1.weights_mine
  17.5 0.1 collective-permute-start.9
  17.5 1.1 %collective-permute-start.5 = (bf16[4,64,768]{2,1,0:T(8,128)(2,1)S(1)}, bf16[4,64,768]{2,1,0:T(8,128)(2,1)S(1)}, u32[]{:S(2)}, u32[]{:S(2)}) collective-permute-start(bf16[4,64,768]{2,1,0:T(8,128)(2,1)S(1)} %collective-permute-done.refs_1_), channel_id=1, source_target_pairs={{0,2},{1,3},{2,4},{3,5},{4,6},{5,7},{6,0},{7,1},{8,10},{9,11},{10,... | collective-permute-start | bytes 1179656 | tf_op jit(solution)/shard_map/ppermute | solution.py:291
  18.7 1.2 %collective-permute-start.6 = (bf16[800,128]{1,0:T(8,128)(2,1)}, bf16[800,128]{1,0:T(8,128)(2,1)S(1)}, u32[]{:S(2)}, u32[]{:S(2)}) collective-permute-start(bf16[800,128]{1,0:T(8,128)(2,1)} %bias.1), channel_id=1, source_target_pairs={{0,8},{8,0},{16,24},{24,16},{1,9},{9,1},{17,25},{25,17},{2,10},{10... | collective-permute-start | bytes 614408 | tf_op jit(solution)/shard_map/ppermute | solution.py:297
  19.9 1.4 %collective-permute-start.7 = (bf16[800,128]{1,0:T(8,128)(2,1)}, bf16[800,128]{1,0:T(8,128)(2,1)S(1)}, u32[]{:S(2)}, u32[]{:S(2)}) collective-permute-start(bf16[800,128]{1,0:T(8,128)(2,1)} %bias.1), channel_id=1, source_target_pairs={{0,16},{8,24},{16,0},{24,8},{1,17},{9,25},{17,1},{25,9},{2,18},{10... | collective-permute-start | bytes 614408 | tf_op jit(solution)/shard_map/ppermute | solution.py:297
  21.3 0.8 %collective-permute-start.8 = (bf16[800,128]{1,0:T(8,128)(2,1)}, bf16[800,128]{1,0:T(8,128)(2,1)S(1)}, u32[]{:S(2)}, u32[]{:S(2)}) collective-permute-start(bf16[800,128]{1,0:T(8,128)(2,1)} %bias.1), channel_id=1, source_target_pairs={{0,24},{8,16},{16,8},{24,0},{1,25},{9,17},{17,9},{25,1},{2,26},{10... | collective-permute-start | bytes 614408 | tf_op jit(solution)/shard_map/ppermute | solution.py:297
  22.2 4.6 %collective-permute-done.6 = bf16[800,128]{1,0:T(8,128)(2,1)S(1)} collective-permute-done((bf16[800,128]{1,0:T(8,128)(2,1)}, bf16[800,128]{1,0:T(8,128)(2,1)S(1)}, u32[]{:S(2)}, u32[]{:S(2)}) %collective-permute-start.6) | collective-permute-done | bytes 204832 | tf_op jit(solution)/shard_map/ppermute | solution.py:297
  26.8 3.6 %collective-permute-done.7 = bf16[800,128]{1,0:T(8,128)(2,1)S(1)} collective-permute-done((bf16[800,128]{1,0:T(8,128)(2,1)}, bf16[800,128]{1,0:T(8,128)(2,1)S(1)}, u32[]{:S(2)}, u32[]{:S(2)}) %collective-permute-start.7) | collective-permute-done | bytes 204832 | tf_op jit(solution)/shard_map/ppermute | solution.py:297
  30.4 1.0 %collective-permute-done.8 = bf16[800,128]{1,0:T(8,128)(2,1)S(1)} collective-permute-done((bf16[800,128]{1,0:T(8,128)(2,1)}, bf16[800,128]{1,0:T(8,128)(2,1)S(1)}, u32[]{:S(2)}, u32[]{:S(2)}) %collective-permute-start.8) | collective-permute-done | bytes 204832 | tf_op jit(solution)/shard_map/ppermute | solution.py:297
  31.4 0.0 collective-permute-done.5.refs_2_
  31.4 0.0 collective-permute-done.9.weights_other
  31.4 1.0 %pad_maximum_fusion.parcel_mine = bf16[4,800,128]{2,1,0:T(8,128)(2,1)S(1)} fusion(bf16[1,800,128]{2,1,0:T(8,128)(2,1)S(1)} %bitcast.16, bf16[1,800,128]{2,1,0:T(8,128)(2,1)S(1)} %bitcast.15, bf16[1,800,128]{2,1,0:T(8,128)(2,1)S(1)} %bitcast.14, bf16[1,800,128]{2,1,0:T(8,128)(2,1)} %bitcast.13), kind=kLoop, calls=%fused_computation | loop fusion | flops 1228800 | bytes 1638400 | tf_op jit(solution)/shard_map/stack | solution.py:369
  32.4 0.1 collective-permute-start.13
  32.5 1.8 %collective-permute-start.14 = (bf16[4,64,768]{2,1,0:T(8,128)(2,1)S(1)}, bf16[4,64,768]{2,1,0:T(8,128)(2,1)S(1)}, u32[]{:S(2)}, u32[]{:S(2)}) collective-permute-start(bf16[4,64,768]{2,1,0:T(8,128)(2,1)S(1)} %collective-permute-done.5.refs_2_), channel_id=1, source_target_pairs={{0,2},{1,3},{2,4},{3,5},{4,6},{5,7},{6,0},{7,1},{8,10},{9,11},{10,... | collective-permute-start | bytes 1179656 | tf_op jit(solution)/shard_map/ppermute | solution.py:291
  34.3 0.0 copy-done.4
  34.3 1.1 %collective-permute-start.10 = (bf16[96,768]{1,0:T(8,128)(2,1)S(1)}, bf16[96,768]{1,0:T(8,128)(2,1)S(1)}, u32[]{:S(2)}, u32[]{:S(2)}) collective-permute-start(bf16[96,768]{1,0:T(8,128)(2,1)S(1)} %copy-done.4), channel_id=1, source_target_pairs={{0,8},{8,0},{16,24},{24,16},{1,9},{9,1},{17,25},{25,17},{2,10},{10... | collective-permute-start | bytes 442376 | tf_op jit(solution)/shard_map/ppermute | solution.py:297
  35.5 1.2 %collective-permute-start.11 = (bf16[96,768]{1,0:T(8,128)(2,1)S(1)}, bf16[96,768]{1,0:T(8,128)(2,1)S(1)}, u32[]{:S(2)}, u32[]{:S(2)}) collective-permute-start(bf16[96,768]{1,0:T(8,128)(2,1)S(1)} %copy-done.4), channel_id=1, source_target_pairs={{0,16},{8,24},{16,0},{24,8},{1,17},{9,25},{17,1},{25,9},{2,18},{10... | collective-permute-start | bytes 442376 | tf_op jit(solution)/shard_map/ppermute | solution.py:297
  36.6 1.2 %collective-permute-start.12 = (bf16[96,768]{1,0:T(8,128)(2,1)S(1)}, bf16[96,768]{1,0:T(8,128)(2,1)S(1)}, u32[]{:S(2)}, u32[]{:S(2)}) collective-permute-start(bf16[96,768]{1,0:T(8,128)(2,1)S(1)} %copy-done.4), channel_id=1, source_target_pairs={{0,24},{8,16},{16,8},{24,0},{1,25},{9,17},{17,9},{25,1},{2,26},{10... | collective-permute-start | bytes 442376 | tf_op jit(solution)/shard_map/ppermute | solution.py:297
  37.8 0.0 copy-done.6
  37.8 0.0 collective-permute-done.13.parcel_other
  37.8 0.0 copy-done.2
  37.8 0.0 copy-done.3
  37.8 7.8 %early.1 = (f32[4,400,128]{2,1,0:T(8,128)S(1)}, bf16[4,384,128]{2,1,0:T(8,128)(2,1)S(1)}, bf16[768,384]{1,0:T(8,128)(2,1)S(1)}, bf16[384,768]{1,0:T(8,128)(2,1)S(1)}) custom-call(bf16[4,96,768]{2,1,0:T(8,128)(2,1)S(1)} %pad_maximum_fusion.1.weights_mine, bf16[4,96,768]{2,1,0:T(8,128)(2,1)S(1)} %collective-permute-done.9.weights_other, ...), custom_call_target="tpu_custom_call" | custom-call | tf_op jit(solution)/shard_map/early/pallas_call | solution.py:377
  45.6 0.2 collective-permute-done.14.block
  45.8 2.8 %late.3 = (f32[1,400,128]{2,1,0:T(8,128)S(1)}, f32[1,400,128]{2,1,0:T(8,128)S(1)}) custom-call(f32[4,400,128]{2,1,0:T(8,128)S(1)} %get-tuple-element.49.partial, bf16[4,384,128]{2,1,0:T(8,128)(2,1)S(1)} %get-tuple-element.50.queries, bf16[768,384]{1,0:T(8,128)(2,1)S(1)} %get-tuple-element.51.key_weight, bf16[384,768]{1,0:T(8,128)(2,1)S(1)} %get-tuple-element.52.value_weight, ...), custom_call_target="tpu_custom_call" | custom-call | tf_op jit(solution)/shard_map/late/pallas_call | solution.py:396
  48.6 0.0 copy-start
  48.6 0.0 copy-start.1
  48.6 0.1 collective-permute-start.16
  48.7 2.8 %late.2 = (f32[1,400,128]{2,1,0:T(8,128)S(1)}, f32[1,400,128]{2,1,0:T(8,128)S(1)}) custom-call(f32[4,400,128]{2,1,0:T(8,128)S(1)} %get-tuple-element.49.partial, bf16[4,384,128]{2,1,0:T(8,128)(2,1)S(1)} %get-tuple-element.50.queries, bf16[768,384]{1,0:T(8,128)(2,1)S(1)} %get-tuple-element.51.key_weight, bf16[384,768]{1,0:T(8,128)(2,1)S(1)} %get-tuple-element.52.value_weight, ...), custom_call_target="tpu_custom_call" | custom-call | tf_op jit(solution)/shard_map/late/pallas_call | solution.py:396
  51.5 0.6 %collective-permute-start.15 = (f32[1,400,128]{2,1,0:T(8,128)S(1)}, f32[1,400,128]{2,1,0:T(8,128)S(1)}, u32[]{:S(2)}, u32[]{:S(2)}) collective-permute-start(f32[1,400,128]{2,1,0:T(8,128)S(1)} %get-tuple-element.55), channel_id=1, source_target_pairs={{0,1},{1,0},{2,3},{3,2},{4,5},{5,4},{6,7},{7,6},{8,9},{9,8},{10,11... | collective-permute-start | bytes 614408 | tf_op jit(solution)/shard_map/ppermute | solution.py:286
  52.0 0.0 collective-permute-done.10
  52.0 0.0 collective-permute-done.11
  52.0 0.0 collective-permute-done.12
  52.0 0.1 pad_maximum_fusion.2.weight_parts
  52.1 0.0 collective-permute-done.16.refs_3_
  52.1 1.0 %collective-permute-done.15.refs_2_ = f32[1,400,128]{2,1,0:T(8,128)S(1)} collective-permute-done((f32[1,400,128]{2,1,0:T(8,128)S(1)}, f32[1,400,128]{2,1,0:T(8,128)S(1)}, u32[]{:S(2)}, u32[]{:S(2)}) %collective-permute-start.15) | collective-permute-done | bytes 204832 | tf_op jit(solution)/shard_map/ppermute | solution.py:286
  53.1 0.0 copy-done
  53.1 0.0 copy-done.1
  53.1 1.2 %finish.1 = bf16[4,64,768]{2,1,0:T(8,128)(2,1)} custom-call(bf16[4,96,768]{2,1,0:T(8,128)(2,1)S(1)} %pad_maximum_fusion.2.weight_parts, bf16[4,64,768]{2,1,0:T(8,128)(2,1)S(1)} %copy-done, bf16[4,64,768]{2,1,0:T(8,128)(2,1)S(1)} %copy-done.1, f32[1,400,128]{2,1,0:T(8,128)S(1)} %get-tuple-element.53.refs_0_, f32[1,400,128]{2,1,0:T(8,128)S(1)} %get-tuple-element.54.refs_1_, ...), custom_call_target="tpu_custom_call" | custom-call | tf_op jit(solution)/shard_map/finish/pallas_call | solution.py:405
  (1 shorter events, 0.0 us)
Async XLA Ops:
  2.9 14.4 %copy-start.5 = (bf16[96,768]{1,0:T(8,128)(2,1)S(1)}, bf16[96,768]{1,0:T(8,128)(2,1)}, u32[]{:S(2)}) copy-start(bf16[96,768]{1,0:T(8,128)(2,1)} %get-tuple-element.37) | copy-start | bytes 442372
  2.9 14.4 %collective-permute-start = (bf16[4,64,768]{2,1,0:T(8,128)(2,1)}, bf16[4,64,768]{2,1,0:T(8,128)(2,1)S(1)}, u32[]{:S(2)}, u32[]{:S(2)}) collective-permute-start(bf16[4,64,768]{2,1,0:T(8,128)(2,1)} %get-tuple-element.31.refs_0_), channel_id=1, source_target_pairs={{0,2},{1,3},{2,4},{3,5},{4,6},{5,7},{6,0},{7,1},{8,10},{9,11},{10,... | collective-permute-start | bytes 1179656 | tf_op jit(solution)/shard_map/ppermute | solution.py:291
  6.0 11.4 %collective-permute-start.4 = (bf16[4,64,768]{2,1,0:T(8,128)(2,1)}, bf16[4,64,768]{2,1,0:T(8,128)(2,1)S(1)}, u32[]{:S(2)}, u32[]{:S(2)}) collective-permute-start(bf16[4,64,768]{2,1,0:T(8,128)(2,1)} %get-tuple-element.33.shifted), channel_id=1, source_target_pairs={{0,1},{1,0},{2,3},{3,2},{4,5},{5,4},{6,7},{7,6},{8,9},{9,8},{10,11... | collective-permute-start | bytes 1179656 | tf_op jit(solution)/shard_map/ppermute | solution.py:286
  6.0 10.4 %collective-permute-start.1 = (bf16[96,768]{1,0:T(8,128)(2,1)}, bf16[96,768]{1,0:T(8,128)(2,1)S(1)}, u32[]{:S(2)}, u32[]{:S(2)}) collective-permute-start(bf16[96,768]{1,0:T(8,128)(2,1)} %get-tuple-element.37), channel_id=1, source_target_pairs={{0,8},{8,0},{16,24},{24,16},{1,9},{9,1},{17,25},{25,17},{2,10},{10... | collective-permute-start | bytes 442376 | tf_op jit(solution)/shard_map/ppermute | solution.py:297
  7.5 9.4 %collective-permute-start.2 = (bf16[96,768]{1,0:T(8,128)(2,1)}, bf16[96,768]{1,0:T(8,128)(2,1)S(1)}, u32[]{:S(2)}, u32[]{:S(2)}) collective-permute-start(bf16[96,768]{1,0:T(8,128)(2,1)} %get-tuple-element.37), channel_id=1, source_target_pairs={{0,16},{8,24},{16,0},{24,8},{1,17},{9,25},{17,1},{25,9},{2,18},{10... | collective-permute-start | bytes 442376 | tf_op jit(solution)/shard_map/ppermute | solution.py:297
  9.0 7.8 %collective-permute-start.3 = (bf16[96,768]{1,0:T(8,128)(2,1)}, bf16[96,768]{1,0:T(8,128)(2,1)S(1)}, u32[]{:S(2)}, u32[]{:S(2)}) collective-permute-start(bf16[96,768]{1,0:T(8,128)(2,1)} %get-tuple-element.37), channel_id=1, source_target_pairs={{0,24},{8,16},{16,8},{24,0},{1,25},{9,17},{17,9},{25,1},{2,26},{10... | collective-permute-start | bytes 442376 | tf_op jit(solution)/shard_map/ppermute | solution.py:297
  9.5 24.8 %copy-start.4 = (bf16[96,768]{1,0:T(8,128)(2,1)S(1)}, bf16[96,768]{1,0:T(8,128)(2,1)}, u32[]{:S(2)}) copy-start(bf16[96,768]{1,0:T(8,128)(2,1)} %param.22) | copy-start | bytes 442372
  9.5 28.3 %copy-start.6 = (bf16[384]{0:T(512)(128)(2,1)S(1)}, bf16[384]{0:T(512)(128)(2,1)}, u32[]{:S(2)}) copy-start(bf16[384]{0:T(512)(128)(2,1)} %param.19) | copy-start | bytes 2308
  9.5 28.3 %copy-start.2 = (bf16[4,64,768]{2,1,0:T(8,128)(2,1)S(1)}, bf16[4,64,768]{2,1,0:T(8,128)(2,1)}, u32[]{:S(2)}) copy-start(bf16[4,64,768]{2,1,0:T(8,128)(2,1)} %get-tuple-element.33.shifted) | copy-start | bytes 1179652
  9.5 28.3 %copy-start.3 = (bf16[4,64,768]{2,1,0:T(8,128)(2,1)S(1)}, bf16[4,64,768]{2,1,0:T(8,128)(2,1)}, u32[]{:S(2)}) copy-start(bf16[4,64,768]{2,1,0:T(8,128)(2,1)} %get-tuple-element.31.refs_0_) | copy-start | bytes 1179652
  17.5 13.9 %collective-permute-start.9 = (bf16[4,96,768]{2,1,0:T(8,128)(2,1)S(1)}, bf16[4,96,768]{2,1,0:T(8,128)(2,1)S(1)}, u32[]{:S(2)}, u32[]{:S(2)}) collective-permute-start(bf16[4,96,768]{2,1,0:T(8,128)(2,1)S(1)} %pad_maximum_fusion.1.weights_mine), channel_id=1, source_target_pairs={{0,1},{1,0},{2,3},{3,2},{4,5},{5,4},{6,7},{7,6},{8,9},{9,8},{10,11... | collective-permute-start | bytes 1769480 | tf_op jit(solution)/shard_map/ppermute | solution.py:286
  17.5 13.9 %collective-permute-start.5 = (bf16[4,64,768]{2,1,0:T(8,128)(2,1)S(1)}, bf16[4,64,768]{2,1,0:T(8,128)(2,1)S(1)}, u32[]{:S(2)}, u32[]{:S(2)}) collective-permute-start(bf16[4,64,768]{2,1,0:T(8,128)(2,1)S(1)} %collective-permute-done.refs_1_), channel_id=1, source_target_pairs={{0,2},{1,3},{2,4},{3,5},{4,6},{5,7},{6,0},{7,1},{8,10},{9,11},{10,... | collective-permute-start | bytes 1179656 | tf_op jit(solution)/shard_map/ppermute | solution.py:291
  18.7 8.1 %collective-permute-start.6 = (bf16[800,128]{1,0:T(8,128)(2,1)}, bf16[800,128]{1,0:T(8,128)(2,1)S(1)}, u32[]{:S(2)}, u32[]{:S(2)}) collective-permute-start(bf16[800,128]{1,0:T(8,128)(2,1)} %bias.1), channel_id=1, source_target_pairs={{0,8},{8,0},{16,24},{24,16},{1,9},{9,1},{17,25},{25,17},{2,10},{10... | collective-permute-start | bytes 614408 | tf_op jit(solution)/shard_map/ppermute | solution.py:297
  19.9 10.5 %collective-permute-start.7 = (bf16[800,128]{1,0:T(8,128)(2,1)}, bf16[800,128]{1,0:T(8,128)(2,1)S(1)}, u32[]{:S(2)}, u32[]{:S(2)}) collective-permute-start(bf16[800,128]{1,0:T(8,128)(2,1)} %bias.1), channel_id=1, source_target_pairs={{0,16},{8,24},{16,0},{24,8},{1,17},{9,25},{17,1},{25,9},{2,18},{10... | collective-permute-start | bytes 614408 | tf_op jit(solution)/shard_map/ppermute | solution.py:297
  21.3 10.0 %collective-permute-start.8 = (bf16[800,128]{1,0:T(8,128)(2,1)}, bf16[800,128]{1,0:T(8,128)(2,1)S(1)}, u32[]{:S(2)}, u32[]{:S(2)}) collective-permute-start(bf16[800,128]{1,0:T(8,128)(2,1)} %bias.1), channel_id=1, source_target_pairs={{0,24},{8,16},{16,8},{24,0},{1,25},{9,17},{17,9},{25,1},{2,26},{10... | collective-permute-start | bytes 614408 | tf_op jit(solution)/shard_map/ppermute | solution.py:297
  32.4 5.4 %collective-permute-start.13 = (bf16[4,800,128]{2,1,0:T(8,128)(2,1)S(1)}, bf16[4,800,128]{2,1,0:T(8,128)(2,1)S(1)}, u32[]{:S(2)}, u32[]{:S(2)}) collective-permute-start(bf16[4,800,128]{2,1,0:T(8,128)(2,1)S(1)} %pad_maximum_fusion.parcel_mine), channel_id=1, source_target_pairs={{0,1},{1,0},{2,3},{3,2},{4,5},{5,4},{6,7},{7,6},{8,9},{9,8},{10,11... | collective-permute-start | bytes 2457608 | tf_op jit(solution)/shard_map/ppermute | solution.py:286
  32.5 13.3 %collective-permute-start.14 = (bf16[4,64,768]{2,1,0:T(8,128)(2,1)S(1)}, bf16[4,64,768]{2,1,0:T(8,128)(2,1)S(1)}, u32[]{:S(2)}, u32[]{:S(2)}) collective-permute-start(bf16[4,64,768]{2,1,0:T(8,128)(2,1)S(1)} %collective-permute-done.5.refs_2_), channel_id=1, source_target_pairs={{0,2},{1,3},{2,4},{3,5},{4,6},{5,7},{6,0},{7,1},{8,10},{9,11},{10,... | collective-permute-start | bytes 1179656 | tf_op jit(solution)/shard_map/ppermute | solution.py:291
  34.3 17.7 %collective-permute-start.10 = (bf16[96,768]{1,0:T(8,128)(2,1)S(1)}, bf16[96,768]{1,0:T(8,128)(2,1)S(1)}, u32[]{:S(2)}, u32[]{:S(2)}) collective-permute-start(bf16[96,768]{1,0:T(8,128)(2,1)S(1)} %copy-done.4), channel_id=1, source_target_pairs={{0,8},{8,0},{16,24},{24,16},{1,9},{9,1},{17,25},{25,17},{2,10},{10... | collective-permute-start | bytes 442376 | tf_op jit(solution)/shard_map/ppermute | solution.py:297
  35.5 16.6 %collective-permute-start.11 = (bf16[96,768]{1,0:T(8,128)(2,1)S(1)}, bf16[96,768]{1,0:T(8,128)(2,1)S(1)}, u32[]{:S(2)}, u32[]{:S(2)}) collective-permute-start(bf16[96,768]{1,0:T(8,128)(2,1)S(1)} %copy-done.4), channel_id=1, source_target_pairs={{0,16},{8,24},{16,0},{24,8},{1,17},{9,25},{17,1},{25,9},{2,18},{10... | collective-permute-start | bytes 442376 | tf_op jit(solution)/shard_map/ppermute | solution.py:297
  36.6 15.4 %collective-permute-start.12 = (bf16[96,768]{1,0:T(8,128)(2,1)S(1)}, bf16[96,768]{1,0:T(8,128)(2,1)S(1)}, u32[]{:S(2)}, u32[]{:S(2)}) collective-permute-start(bf16[96,768]{1,0:T(8,128)(2,1)S(1)} %copy-done.4), channel_id=1, source_target_pairs={{0,24},{8,16},{16,8},{24,0},{1,25},{9,17},{17,9},{25,1},{2,26},{10... | collective-permute-start | bytes 442376 | tf_op jit(solution)/shard_map/ppermute | solution.py:297
  48.6 4.5 %copy-start = (bf16[4,64,768]{2,1,0:T(8,128)(2,1)S(1)}, bf16[4,64,768]{2,1,0:T(8,128)(2,1)}, u32[]{:S(2)}) copy-start(bf16[4,64,768]{2,1,0:T(8,128)(2,1)} %activations.1) | copy-start | bytes 1179652
  48.6 4.5 %copy-start.1 = (bf16[4,64,768]{2,1,0:T(8,128)(2,1)S(1)}, bf16[4,64,768]{2,1,0:T(8,128)(2,1)}, u32[]{:S(2)}) copy-start(bf16[4,64,768]{2,1,0:T(8,128)(2,1)} %output_gate.1) | copy-start | bytes 1179652
  48.6 3.5 %collective-permute-start.16 = (f32[1,400,128]{2,1,0:T(8,128)S(1)}, f32[1,400,128]{2,1,0:T(8,128)S(1)}, u32[]{:S(2)}, u32[]{:S(2)}) collective-permute-start(f32[1,400,128]{2,1,0:T(8,128)S(1)} %get-tuple-element.56), channel_id=1, source_target_pairs={{0,1},{1,0},{2,3},{3,2},{4,5},{5,4},{6,7},{7,6},{8,9},{9,8},{10,11... | collective-permute-start | bytes 614408 | tf_op jit(solution)/shard_map/ppermute | solution.py:286
  51.5 1.6 %collective-permute-start.15 = (f32[1,400,128]{2,1,0:T(8,128)S(1)}, f32[1,400,128]{2,1,0:T(8,128)S(1)}, u32[]{:S(2)}, u32[]{:S(2)}) collective-permute-start(f32[1,400,128]{2,1,0:T(8,128)S(1)} %get-tuple-element.55), channel_id=1, source_target_pairs={{0,1},{1,0},{2,3},{3,2},{4,5},{5,4},{6,7},{7,6},{8,9},{9,8},{10,11... | collective-permute-start | bytes 614408 | tf_op jit(solution)/shard_map/ppermute | solution.py:286
where the time goes:
time: 54.5 us; the launch traced here: 54.3 us
  Pallas kernels  24.4 us (45%)
  starting transfers between devices  17.3 us (32%)
  waiting for transfers between devices  11.3 us (21%)
  other arithmetic  1.19 us (2%)
    ppermute x9, starting transfers between devices, from_noise(): lax.ppermute(array, 'noise', [(i, i ^ k) for i in range(lax.axis_size('no...  10.5 us
    ppermute x9, waiting for transfers between devices, from_noise(): lax.ppermute(array, 'noise', [(i, i ^ k) for i in range(lax.axis_size('no...  9.61 us
    pallas_call x1, Pallas kernels, body(): pl.pallas_call(functools.partial(early_kernel, steps, heads), out_shape=[...  7.8 us
    pallas_call x1, Pallas kernels, body(): pl.pallas_call(bias_kernel, in_specs=[in_hbm, in_hbm, pl.BlockSpec(memory...  6.94 us
    ppermute x3, starting transfers between devices, next_chip(): lax.ppermute(array, 'row', [(i, (i + 2) % size) for i in range(size)])  6.03 us
    pallas_call x2, Pallas kernels, body(): pl.pallas_call(functools.partial(late_kernel, steps, heads, c * each), ou...  5.51 us
    pallas_call x1, Pallas kernels, body(): pl.pallas_call(shift_kernel, in_specs=[in_hbm] * 6, out_shape=[struct(act...  2.93 us
    pallas_call x1, Pallas kernels, body(): pl.pallas_call(functools.partial(finish_kernel, heads, chunks), out_shape...  1.22 us
  transfers between devices with their start and end apart: 17, of which 7 were waited for; matrix products, arithmetic and copies ran while one was open for 0% of the time, Pallas kernels for 37%

commit v1 on v0

--- a/solution.py
+++ b/solution.py
@@ -85,28 +85,43 @@
     copies.append(pltpu.make_async_copy(value_hbm, value_weight, sems.at[pieces]))
     for copy in copies:
         copy.start()
-    twice = jnp.concatenate([weights[...], weights[...]], axis=1)
+    record = 2 * heads
+    extended = jnp.concatenate(
+        [weights[...], jnp.full((heads, channels), 1.0 / channels, jnp.bfloat16)], axis=0
+    )
+    square = (channels, channels)
+    diagonal = lax.broadcasted_iota(jnp.int32, square, 0) == lax.broadcasted_iota(jnp.int32, square, 1)
+    centring = (jnp.where(diagonal, 1.0, 0.0) - 1.0 / channels).astype(jnp.bfloat16)
+    lane = lax.broadcasted_iota(jnp.int32, (1, rows), 1)
+    squares = jnp.zeros((columns, rows), jnp.float32)
     for i in range(pieces):
         copies[i].wait()
-        normed = layer_norm(pair[i].reshape(per * columns, channels).astype(jnp.float32))
-        upper = normed.astype(jnp.bfloat16)
-        lower = (normed - upper.astype(jnp.float32)).astype(jnp.bfloat16)
+        block = pair[i].reshape(per * columns, channels)
+        centred = jnp.dot(block, centring, preferred_element_type=jnp.float32)
+        summed = jnp.sum(centred * centred, axis=1, keepdims=True)
         result = lax.dot_general(
-            twice,
-            jnp.concatenate([upper, lower], axis=1),
-            (((1,), (1,)), ((), ())),
-            preferred_element_type=jnp.float32,
+            extended, block, (((1,), (1,)), ((), ())), preferred_element_type=jnp.float32
         )
         for r in range(per):
-            at = (i * per + r) * heads
-            collected[at : at + heads, :] = result[:, r * columns : (r + 1) * columns]
+            row = i * per + r
+            collected[row * record : (row + 1) * record, :] = result[:, r * columns : (r + 1) * columns]
+            squares = jnp.where(lane == row, summed[r * columns : (r + 1) * columns], squares)
     core = lax.rem(lax.axis_index("row"), 2)
     half = columns // 2
-    for h in range(heads):
-        turned = collected[pl.ds(h, rows, stride=heads), :].T
-        low, up = turned[:half], turned[half:]
-        both = [jnp.where(core == 0, low, up), jnp.where(core == 0, up, low)]
-        parcel[h * half : (h + 1) * half, :] = jnp.concatenate(both, axis=1).astype(jnp.bfloat16)
+    average = collected[pl.ds(heads, rows, stride=record), :].T
+    inverse = lax.rsqrt(squares / channels + epsilon)
+    for p in range(heads // 2):
+        own, other = [], []
+        for h in (2 * p, 2 * p + 1):
+            summed = jnp.sum(weights[h : h + 1, :].astype(jnp.float32), axis=1, keepdims=True)
+            turned = (collected[pl.ds(h, rows, stride=record), :].T - average * summed) * inverse
+            low, up = turned[:half], turned[half:]
+            own.append(jnp.where(core == 0, low, up))
+            other.append(jnp.where(core == 0, up, low))
+        at = p * half
+        parcel[at : at + half, :] = jnp.concatenate(own, axis=1).astype(jnp.bfloat16)
+        at += heads // 2 * half
+        parcel[at : at + half, :] = jnp.concatenate(other[::-1], axis=1).astype(jnp.bfloat16)
     copies[pieces].wait()
     depth, breadth = value_weight.shape
     whole = value_weight[...].astype(jnp.float32)
@@ -116,88 +131,107 @@
         parcel[at : at + depth // 2, :] = kept[:, t * columns : (t + 1) * columns]
 
 
-def attend_keys(heads, keys, values, penalty, bias_of, queries):
-    width = queries.shape[0] // heads
+def spread_queries(heads, queries, spread):
+    count, head_features = queries.shape
+    width = head_features // heads
+    lane = lax.broadcasted_iota(jnp.int32, (1, head_features), 1)
+    one = (lax.broadcasted_iota(jnp.int32, (count, 128), 1) == 0).astype(jnp.bfloat16)
+    turned = jnp.concatenate([queries[count // 2 :], queries[: count // 2]], axis=0)
+    for h in range(heads):
+        inside = ((lane >= h * width) & (lane < (h + 1) * width)).astype(jnp.bfloat16)
+        spread[h * count : (h + 1) * count, 0:head_features] = (turned if h % 2 else queries) * inside
+        spread[h * count : (h + 1) * count, head_features:] = one
+
+
+def attend_keys(heads, tokens, keys, values, bias_of, spread):
+    width = values.shape[0] // heads
+    count = spread.shape[0] // heads
+    penalty = jnp.where(tokens[:, 0:1].astype(jnp.float32) > absent / 2, masked_score, 0.0)
+    penalty = jnp.broadcast_to(penalty, (tokens.shape[0], 128)).astype(jnp.bfloat16)
+    scores = lax.dot_general(
+        jnp.concatenate([keys, penalty], axis=1),
+        spread[...],
+        (((1,), (1,)), ((), ())),
+        preferred_element_type=jnp.float32,
+    ) * (log2_e / math.sqrt(width))
     sums, highs, totals = [], [], []
     for h in range(heads):
-        across = slice(h * width, (h + 1) * width)
-        score = jnp.dot(keys[:, across], queries[across, :], preferred_element_type=jnp.float32)
-        score = score * (log2_e / math.sqrt(width)) + (bias_of(h) * log2_e + penalty)
+        score = scores[:, h * count : (h + 1) * count] + bias_of(h) * log2_e
         high = jnp.max(score, axis=0, keepdims=True)
         probs = jnp.exp2(score - high)
         totals.append(jnp.sum(probs, axis=0, keepdims=True))
         highs.append(high)
         sums.append(
-            jnp.dot(values[across, :], probs.astype(jnp.bfloat16), preferred_element_type=jnp.float32)
+            jnp.dot(
+                values[h * width : (h + 1) * width],
+                probs.astype(jnp.bfloat16),
+                preferred_element_type=jnp.float32,
+            )
         )
     return sums, highs, totals
 
 
-def absent_penalty(tokens):
-    return jnp.where(tokens[:, 0:1].astype(jnp.float32) > absent / 2, masked_score, 0.0)
-
-
-def bias_picker(parcel_mine, parcel_other, steps, first, rows):
+def bias_picker(parcel, swapped, steps, first, rows):
     chip = lax.axis_index("row") // 2
     place = lax.axis_index("noise")
-    own = lax.broadcasted_iota(jnp.int32, (1, 2 * rows), 1) < rows
+    left = lax.broadcasted_iota(jnp.int32, (1, 2 * rows), 1) < rows
 
     def pick(b, h):
         part = lax.rem(chip - (first + b) + steps, steps) ^ place
-        at = slice(h * rows, (h + 1) * rows)
-        return jnp.where(own, parcel_mine[part, at].astype(jnp.float32), parcel_other[part, at].astype(jnp.float32))
+        at = slice(h // 2 * rows, (h // 2 + 1) * rows)
+        pairs = parcel[part, at].astype(jnp.float32), swapped[part, at].astype(jnp.float32)
+        return jnp.where(left, pairs[h % 2], pairs[1 - h % 2])
 
     return pick
 
 
-def early_kernel(
-    steps, heads, weights_mine, weights_other, query_bias, shifted, shifted_other, parcel_mine, parcel_other, *refs
-):
+def early_kernel(steps, heads, weights_mine, weights_other, query_bias, shifted, parcel, swapped, swapped_value, *refs):
     blocks = refs[: steps - 1]
-    partial, queries, key_weight, value_weight, full, full_value = refs[steps - 1 :]
-    noise_size, half, _ = weights_mine.shape
+    partial, queries, key_weight, value_weight, full, full_value, spread = refs[steps - 1 :]
     samples, rows, features = shifted.shape
+    noise_size, half = swapped_value.shape[0], weights_mine.shape[1] - rows * samples // swapped_value.shape[0]
     breadth = key_weight.shape[1]
     width = breadth // heads
     core = lax.rem(lax.axis_index("row"), 2)
     place = lax.axis_index("noise")
-    for part, parcel, of_core in (
-        (weights_mine, parcel_mine, core),
-        (weights_other, parcel_other, 1 - core),
+    below = parcel.shape[1] - breadth // 128 * half
+    for part, value, skipped, of_core in (
+        (weights_mine, parcel, below, core),
+        (weights_other, swapped_value, 0, 1 - core),
     ):
         for k in range(noise_size):
             start = ((place ^ k) * 2 + of_core) * half
             down = pl.ds(pl.multiple_of(start, math.gcd(half, 32)), half)
-            full[down, :] = part[k].astype(full.dtype)
+            full[down, :] = part[k, 0:half].astype(full.dtype)
             for t in range(breadth // 128):
-                at = heads * rows + t * half
-                full_value[down, t * 128 : (t + 1) * 128] = parcel[k, at : at + half].astype(full.dtype)
+                at = skipped + t * half
+                full_value[down, t * 128 : (t + 1) * 128] = value[k, at : at + half].astype(full.dtype)
     key_weight[...] = full[:, breadth : 2 * breadth].astype(jnp.bfloat16)
     value_weight[...] = full_value[...].astype(jnp.float32).T.astype(jnp.bfloat16)
-    sides = []
-    for tokens in (shifted, shifted_other):
+    for side, tokens in enumerate((shifted[...], weights_other[:, half:])):
         result = jnp.dot(
-            tokens[...].reshape(samples * rows, features),
+            tokens.reshape(samples * rows, features),
             full[:, 0:breadth].astype(jnp.bfloat16),
             preferred_element_type=jnp.float32,
         ) + query_bias[...].astype(jnp.float32)
-        sides.append(result.astype(jnp.bfloat16).astype(jnp.float32))
-    pick = bias_picker(parcel_mine, parcel_other, steps, 0, rows)
+        queries[:, side * rows : (side + 1) * rows] = result.astype(jnp.bfloat16).reshape(
+            samples, rows, breadth
+        )
+    pick = bias_picker(parcel, swapped, steps, 0, rows)
     for s in range(samples):
-        both = [side[s * rows : (s + 1) * rows] for side in sides]
-        queries[s] = jnp.concatenate(both, axis=0).T.astype(jnp.bfloat16)
         tokens = jnp.concatenate([block[s] for block in blocks], axis=0)
         keys = jnp.dot(tokens, key_weight[...], preferred_element_type=jnp.float32).astype(jnp.bfloat16)
         values = lax.dot_general(
             value_weight[...], tokens, (((1,), (1,)), ((), ())), preferred_element_type=jnp.float32
         ).astype(jnp.bfloat16)
+        spread_queries(heads, queries[s], spread)
         sums, highs, totals = attend_keys(
             heads,
+            tokens,
             keys,
             values,
-            absent_penalty(tokens),
             lambda h: jnp.concatenate([pick(b, h) for b in range(steps - 1)], axis=0),
-            queries.at[s],
+            spread,
         )
         for h in range(heads):
             partial[s, h * width : (h + 1) * width] = sums[h]
@@ -205,30 +239,20 @@
             partial[s, breadth + heads + h : breadth + heads + h + 1] = totals[h]
 
 
-def late_kernel(
-    steps, heads, first, partial, queries, key_weight, value_weight, parcel_mine, parcel_other, block, keep, give, merged
-):
+def late_kernel(steps, heads, first, partial, queries, key_weight, value_weight, parcel, swapped, block, keep, give, merged, spread):
     samples = merged.shape[0]
-    _, rows, features = block.shape
+    rows = block.shape[1]
     breadth = key_weight.shape[1]
     width = breadth // heads
-    pick = bias_picker(parcel_mine, parcel_other, steps, steps - 1, rows)
-    tokens = block[first : first + samples].reshape(samples * rows, features)
-    all_keys = jnp.dot(tokens, key_weight[...], preferred_element_type=jnp.float32).astype(jnp.bfloat16)
-    all_values = lax.dot_general(
-        value_weight[...], tokens, (((1,), (1,)), ((), ())), preferred_element_type=jnp.float32
-    ).astype(jnp.bfloat16)
-    penalty = absent_penalty(tokens)
+    pick = bias_picker(parcel, swapped, steps, steps - 1, rows)
     for s in range(samples):
-        here = slice(s * rows, (s + 1) * rows)
-        sums, highs, totals = attend_keys(
-            heads,
-            all_keys[here],
-            all_values[:, here],
-            penalty[here],
-            lambda h: pick(0, h),
-            queries.at[first + s],
-        )
+        tokens = block[first + s]
+        keys = jnp.dot(tokens, key_weight[...], preferred_element_type=jnp.float32).astype(jnp.bfloat16)
+        values = lax.dot_general(
+            value_weight[...], tokens, (((1,), (1,)), ((), ())), preferred_element_type=jnp.float32
+        ).astype(jnp.bfloat16)
+        spread_queries(heads, queries[first + s], spread)
+        sums, highs, totals = attend_keys(heads, tokens, keys, values, lambda h: pick(0, h), spread)
         before = partial.at[first + s]
         for h in range(heads):
             at_high = slice(breadth + h, breadth + h + 1)
@@ -241,10 +265,15 @@
             merged[s, at_total] = before[at_total] * old + totals[h] * new
     half = merged.shape[2] // 2
     left = lax.broadcasted_iota(jnp.int32, (1, 2 * half), 1) < half
+    row = lax.broadcasted_iota(jnp.int32, (merged.shape[1], 1), 0)
+    head = jnp.where(row < breadth, row // width, (row - breadth) % heads)
+    even = head % 2 == 0
     for pair in range(samples // 2):
         a, b = merged[2 * pair], merged[2 * pair + 1]
-        keep[pair] = jnp.where(left, a, pltpu.roll(b, half, 1))
-        give[pair] = jnp.where(left, pltpu.roll(a, half, 1), b)
+        lefts = jnp.where(left, a, pltpu.roll(b, half, 1))
+        rights = jnp.where(left, pltpu.roll(a, half, 1), b)
+        keep[pair] = jnp.where(even, lefts, rights)
+        give[pair] = jnp.where(even, rights, lefts)
 
 
 def finish_kernel(heads, chunks, weight_parts, activations, output_gate, *refs):
@@ -338,57 +367,67 @@
 
     ring = [sent, next_chip(sent)]
     weights = [from_noise(packed, k) for k in range(noise_size)]
-    shifted_other = swap_cores(shifted)
     pair_repr, _ = after((pair_repr, packed))
     pieces = 8
     columns, channels = pair_repr.shape[1:]
+    tile_rows = heads * rows
     parcel = pl.pallas_call(
         bias_kernel,
         in_specs=[in_hbm, in_hbm, pl.BlockSpec(memory_space=pltpu.VMEM)],
-        out_shape=struct((heads * rows + 3 * half, columns), bf16),
+        out_shape=struct((tile_rows + 3 * half, columns), bf16),
         scratch_shapes=[
             pltpu.VMEM((pieces, rows // pieces, columns, channels), bf16),
             pltpu.VMEM(value_weight.shape, bf16),
-            pltpu.VMEM((rows * heads, columns), f32),
+            pltpu.VMEM((rows * 2 * heads, columns), f32),
             pltpu.SemaphoreType.DMA((pieces + 1,)),
         ],
         compiler_params=pltpu.CompilerParams(vmem_limit_bytes=wide_bytes),
         name="bias",
     )(pair_repr, value_weight, bias_weight.T)
 
-    ring[1], weights, shifted_other, parcel = after((ring[1], weights, shifted_other, parcel))
+    ring[1], weights, parcel = after((ring[1], weights, parcel))
     ring.append(next_chip(ring[1]))
-    weights_mine = jnp.stack(weights)
+    tokens = shifted.reshape(noise_size, samples * rows // noise_size, features)
+    weights_mine = jnp.concatenate([jnp.stack(weights), tokens], axis=1)
     weights_other = swap_cores(weights_mine)
     parcels = [from_noise(parcel, k) for k in range(noise_size)]
 
-    ring[2], parcels, weights_other, output_weight = after((ring[2], parcels, weights_other, output_weight))
     for _ in range(steps - 3):
         ring.append(next_chip(ring[-1]))
     last = ring.pop()
+    parcels, _ = after((parcels, ring[2]))
     parcel_mine = jnp.stack(parcels)
-    parcel_other = swap_cores(parcel_mine)
-    output_parts = jnp.stack([from_noise(output_weight, k) for k in range(noise_size)])
+    swapped = swap_cores(parcel_mine[:, tile_rows // 2 : tile_rows])
+    swapped_value = swap_cores(parcel_mine[:, tile_rows:])
+    output_weight, _ = after((output_weight, ring[2]))
+    output_parts = [output_weight]
+    for k in range(noise_size.bit_length() - 1):
+        mine = jnp.stack(output_parts)
+        theirs = from_noise(mine, 2**k)
+        output_parts += [theirs[i] for i in range(2**k)]
+    output_parts = jnp.stack(output_parts)
 
     bias_row = query_bias.reshape(1, head_features)
     record = head_features + 2 * heads
     full_type = f32 if half % 16 else bf16
     output_type = f32 if output_weight.shape[0] % 16 else bf16
+    spread = pltpu.VMEM((heads * 2 * rows, head_features + 128), bf16)
     partial, queries, key_full, value_full = pl.pallas_call(
         functools.partial(early_kernel, steps, heads),
         out_shape=[
             struct((samples, record, 2 * rows), f32),
-            struct((samples, head_features, 2 * rows), bf16),
+            struct((samples, 2 * rows, head_features), bf16),
             struct((features, head_features), bf16),
             struct((head_features, features), bf16),
         ],
         scratch_shapes=[
             pltpu.VMEM((features, 2 * head_features), full_type),
             pltpu.VMEM((features, head_features), full_type),
+            spread,
         ],
         compiler_params=params,
         name="early",
-    )(weights_mine, weights_other, bias_row, shifted, shifted_other, parcel_mine, parcel_other, *ring)
+    )(weights_mine, weights_other, bias_row, shifted, parcel_mine, swapped, swapped_value, *ring)
     keep, got = [], []
     chunks = 2
     each = samples // chunks
@@ -396,10 +435,10 @@
         kept, give = pl.pallas_call(
             functools.partial(late_kernel, steps, heads, c * each),
             out_shape=[struct((each // 2, record, 2 * rows), f32)] * 2,
-            scratch_shapes=[pltpu.VMEM((each, record, 2 * rows), f32)],
+            scratch_shapes=[pltpu.VMEM((each, record, 2 * rows), f32), spread],
             compiler_params=params,
             name="late",
-        )(partial, queries, key_full, value_full, parcel_mine, parcel_other, last)
+        )(partial, queries, key_full, value_full, parcel_mine, swapped, last)
         keep.append(kept)
         got.append(swap_cores(give))
     return pl.pallas_call(

time: 54.5 us -> 51.5 us (0.945)
  waiting for transfers between devices: 11.3 us -> 17.6 us
  Pallas kernels: 24.4 us -> 18.3 us
  starting transfers between devices: 17.3 us -> 14.9 us
  other arithmetic: 1.19 us -> 0.26 us
    ppermute x3, waiting for transfers between devices: 0.69 us -> 13 us  [next_chip(): lax.ppermute(array, 'row', [(i, (i + 2) % size) for i in range(size)])]
    ppermute x9 -> x8, waiting for transfers between devices: 9.61 us -> 3.57 us  [from_noise(): lax.ppermute(array, 'noise', [(i, i ^ k) for i in range(lax.axis_size('no...]
    pallas_call x1, Pallas kernels: 7.8 us -> 4.72 us  [body(): pl.pallas_call(functools.partial(early_kernel, steps, heads), out_shape=[...]
    ppermute x3, starting transfers between devices: 6.03 us -> 3.62 us  [next_chip(): lax.ppermute(array, 'row', [(i, (i + 2) % size) for i in range(size)])]
    pallas_call x2, Pallas kernels: 5.51 us -> 3.53 us  [body(): pl.pallas_call(functools.partial(late_kernel, steps, heads, c * each), ou...]
    pallas_call x1, Pallas kernels: 6.94 us -> 5.85 us  [body(): pl.pallas_call(bias_kernel, in_specs=[in_hbm, in_hbm, pl.BlockSpec(memory...]
    another operation x1, other arithmetic: 1.04 us -> 0.11 us  [body(): parcel_mine = jnp.stack(parcels)]
    ppermute x9 -> x8, starting transfers between devices: 10.5 us -> 10.1 us  [from_noise(): lax.ppermute(array, 'noise', [(i, i ^ k) for i in range(lax.axis_size('no...]
  transfers between devices with their start and end apart: 17 -> 16, of which waited for: 7 -> 6; matrix products, arithmetic and copies ran while one was open for 0% -> 0% of each run, Pallas kernels for 37% -> 27%
where the time goes in v1:
time: 51.5 us; the launch traced here: 51.3 us
  Pallas kernels  18.3 us (36%)
  waiting for transfers between devices  17.6 us (34%)
  starting transfers between devices  14.9 us (29%)
    ppermute x3, waiting for transfers between devices, next_chip(): lax.ppermute(array, 'row', [(i, (i + 2) % size) for i in range(size)])  13 us
    ppermute x8, starting transfers between devices, from_noise(): lax.ppermute(array, 'noise', [(i, i ^ k) for i in range(lax.axis_size('no...  10.1 us
    pallas_call x1, Pallas kernels, body(): pl.pallas_call(bias_kernel, in_specs=[in_hbm, in_hbm, pl.BlockSpec(memory...  5.85 us
    pallas_call x1, Pallas kernels, body(): pl.pallas_call(functools.partial(early_kernel, steps, heads), out_shape=[...  4.72 us
    ppermute x3, starting transfers between devices, next_chip(): lax.ppermute(array, 'row', [(i, (i + 2) % size) for i in range(size)])  3.62 us
    ppermute x8, waiting for transfers between devices, from_noise(): lax.ppermute(array, 'noise', [(i, i ^ k) for i in range(lax.axis_size('no...  3.57 us
    pallas_call x2, Pallas kernels, body(): pl.pallas_call(functools.partial(late_kernel, steps, heads, c * each), ou...  3.53 us
    pallas_call x1, Pallas kernels, body(): pl.pallas_call(shift_kernel, in_specs=[in_hbm] * 6, out_shape=[struct(act...  2.93 us
  transfers between devices with their start and end apart: 16, of which 6 were waited for; matrix products, arithmetic and copies ran while one was open for 0% of the time, Pallas kernels for 27%

profile of v1, /device:TPU:0, one launch (start us, length us, event | category | flops | bytes accessed | tf_op | source)
XLA Modules:
  0.0 51.3 jit_solution(485995404907440248)
XLA Ops:
  0.0 2.9 %shift.1 = (bf16[4,64,768]{2,1,0:T(8,128)(2,1)}, bf16[4,64,768]{2,1,0:T(8,128)(2,1)}, bf16[96,768]{1,0:T(8,128)(2,1)}) custom-call(bf16[4,64,768]{2,1,0:T(8,128)(2,1)} %activations.1, bf16[4,64,768]{2,1,0:T(8,128)(2,1)} %scale_hbm.1, bf16[4,64,768]{2,1,0:T(8,128)(2,1)} %shift_hbm.1, s32[4,64]{1,0:T(4,128)} %mask_hbm.1, bf16[192,384]{1,0:T(8,128)(2,1)} %query_hbm.1, ...), custom_call_target="tpu_custom_call" | custom-call | tf_op jit(solution)/shard_map/shift/pallas_call | solution.py:356
  2.9 0.0 copy-start.1
  3.0 0.0 copy-start.6
  3.0 3.1 %collective-permute-start = (bf16[4,64,768]{2,1,0:T(8,128)(2,1)}, bf16[4,64,768]{2,1,0:T(8,128)(2,1)S(1)}, u32[]{:S(2)}, u32[]{:S(2)}) collective-permute-start(bf16[4,64,768]{2,1,0:T(8,128)(2,1)} %get-tuple-element.28.refs_0_), channel_id=1, source_target_pairs={{0,2},{1,3},{2,4},{3,5},{4,6},{5,7},{6,0},{7,1},{8,10},{9,11},{10,... | collective-permute-start | bytes 1179656 | tf_op jit(solution)/shard_map/ppermute | solution.py:320
  6.0 1.5 %collective-permute-start.1 = (bf16[96,768]{1,0:T(8,128)(2,1)}, bf16[96,768]{1,0:T(8,128)(2,1)S(1)}, u32[]{:S(2)}, u32[]{:S(2)}) collective-permute-start(bf16[96,768]{1,0:T(8,128)(2,1)} %get-tuple-element.33), channel_id=1, source_target_pairs={{0,8},{8,0},{16,24},{24,16},{1,9},{9,1},{17,25},{25,17},{2,10},{10... | collective-permute-start | bytes 442376 | tf_op jit(solution)/shard_map/ppermute | solution.py:326
  7.5 1.5 %collective-permute-start.2 = (bf16[96,768]{1,0:T(8,128)(2,1)}, bf16[96,768]{1,0:T(8,128)(2,1)S(1)}, u32[]{:S(2)}, u32[]{:S(2)}) collective-permute-start(bf16[96,768]{1,0:T(8,128)(2,1)} %get-tuple-element.33), channel_id=1, source_target_pairs={{0,16},{8,24},{16,0},{24,8},{1,17},{9,25},{17,1},{25,9},{2,18},{10... | collective-permute-start | bytes 442376 | tf_op jit(solution)/shard_map/ppermute | solution.py:326
  9.1 0.5 collective-permute-start.3
  9.5 0.0 copy-start.5
  9.5 5.9 %bias.1 = bf16[800,128]{1,0:T(8,128)(2,1)} custom-call(bf16[64,128,128]{2,1,0:T(8,128)(2,1)} %pair_hbm, bf16[192,384]{1,0:T(8,128)(2,1)} %value_hbm.1, bf16[8,128]{1,0:T(8,128)(2,1)} %bitcast.21), custom_call_target="tpu_custom_call" | custom-call | tf_op jit(solution)/shard_map/bias/pallas_call | solution.py:374
  15.4 0.0 copy-start.4
  15.4 0.0 collective-permute-done.1
  15.4 0.6 %collective-permute-done.2 = bf16[96,768]{1,0:T(8,128)(2,1)S(1)} collective-permute-done((bf16[96,768]{1,0:T(8,128)(2,1)}, bf16[96,768]{1,0:T(8,128)(2,1)S(1)}, u32[]{:S(2)}, u32[]{:S(2)}) %collective-permute-start.2) | collective-permute-done | bytes 147488 | tf_op jit(solution)/shard_map/ppermute | solution.py:326
  16.0 0.0 collective-permute-done.3
  16.0 1.3 %collective-permute-done.refs_1_ = bf16[4,64,768]{2,1,0:T(8,128)(2,1)S(1)} collective-permute-done((bf16[4,64,768]{2,1,0:T(8,128)(2,1)}, bf16[4,64,768]{2,1,0:T(8,128)(2,1)S(1)}, u32[]{:S(2)}, u32[]{:S(2)}) %collective-permute-start) | collective-permute-done | bytes 393248 | tf_op jit(solution)/shard_map/ppermute | solution.py:320
  17.4 0.0 copy-done.1
  17.4 0.0 copy-done.6
  17.4 0.1 pad_maximum_fusion.weights_mine
  17.5 0.0 copy-start.7
  17.5 0.0 copy-start.3
  17.5 0.1 collective-permute-start.7
  17.6 0.3 collective-permute-start.4
  17.9 0.0 copy-done.4
  17.9 2.3 %collective-permute-start.10 = (bf16[800,128]{1,0:T(8,128)(2,1)S(1)}, bf16[800,128]{1,0:T(8,128)(2,1)S(1)}, u32[]{:S(2)}, u32[]{:S(2)}) collective-permute-start(bf16[800,128]{1,0:T(8,128)(2,1)S(1)} %copy-done.4), channel_id=1, source_target_pairs={{0,24},{8,16},{16,8},{24,0},{1,25},{9,17},{17,9},{25,1},{2,26},{10... | collective-permute-start | bytes 614408 | tf_op jit(solution)/shard_map/ppermute | solution.py:326
  20.2 0.6 %collective-permute-start.8 = (bf16[800,128]{1,0:T(8,128)(2,1)S(1)}, bf16[800,128]{1,0:T(8,128)(2,1)S(1)}, u32[]{:S(2)}, u32[]{:S(2)}) collective-permute-start(bf16[800,128]{1,0:T(8,128)(2,1)S(1)} %copy-done.4), channel_id=1, source_target_pairs={{0,8},{8,0},{16,24},{24,16},{1,9},{9,1},{17,25},{25,17},{2,10},{10... | collective-permute-start | bytes 614408 | tf_op jit(solution)/shard_map/ppermute | solution.py:326
  20.7 0.6 %collective-permute-start.9 = (bf16[800,128]{1,0:T(8,128)(2,1)S(1)}, bf16[800,128]{1,0:T(8,128)(2,1)S(1)}, u32[]{:S(2)}, u32[]{:S(2)}) collective-permute-start(bf16[800,128]{1,0:T(8,128)(2,1)S(1)} %copy-done.4), channel_id=1, source_target_pairs={{0,16},{8,24},{16,0},{24,8},{1,17},{9,25},{17,1},{25,9},{2,18},{10... | collective-permute-start | bytes 614408 | tf_op jit(solution)/shard_map/ppermute | solution.py:326
  21.4 9.5 %collective-permute-done.4.refs_2_ = bf16[4,64,768]{2,1,0:T(8,128)(2,1)S(1)} collective-permute-done((bf16[4,64,768]{2,1,0:T(8,128)(2,1)S(1)}, bf16[4,64,768]{2,1,0:T(8,128)(2,1)S(1)}, u32[]{:S(2)}, u32[]{:S(2)}) %collective-permute-start.4) | collective-permute-done | bytes 393248 | tf_op jit(solution)/shard_map/ppermute | solution.py:320
  30.9 0.0 copy-done.5
  30.9 1.5 %collective-permute-start.5 = (bf16[1,96,768]{2,1,0:T(8,128)(2,1)S(1)}, bf16[1,96,768]{2,1,0:T(8,128)(2,1)S(1)}, u32[]{:S(2)}, u32[]{:S(2)}) collective-permute-start(bf16[1,96,768]{2,1,0:T(8,128)(2,1)S(1)} %bitcast.11), channel_id=1, source_target_pairs={{0,8},{8,0},{16,24},{24,16},{1,9},{9,1},{17,25},{25,17},{2,10},{10... | collective-permute-start | bytes 442376 | tf_op jit(solution)/shard_map/ppermute | solution.py:326
  32.4 0.0 collective-permute-done.10
  32.4 0.0 collective-permute-done.8
  32.4 0.0 collective-permute-done.9
  32.4 0.2 collective-permute-start.13
  32.6 0.1 pad_maximum_fusion.1.parcel
  32.8 0.1 collective-permute-start.12
  32.9 0.5 collective-permute-start.11
  33.4 2.9 %collective-permute-done.5 = bf16[1,96,768]{2,1,0:T(8,128)(2,1)S(1)} collective-permute-done((bf16[1,96,768]{2,1,0:T(8,128)(2,1)S(1)}, bf16[1,96,768]{2,1,0:T(8,128)(2,1)S(1)}, u32[]{:S(2)}, u32[]{:S(2)}) %collective-permute-start.5) | collective-permute-done | bytes 147488 | tf_op jit(solution)/shard_map/ppermute | solution.py:326
  36.3 1.6 %collective-permute-start.6 = (bf16[2,96,768]{2,1,0:T(8,128)(2,1)S(1)}, bf16[2,96,768]{2,1,0:T(8,128)(2,1)S(1)}, u32[]{:S(2)}, u32[]{:S(2)}) collective-permute-start(bf16[2,96,768]{2,1,0:T(8,128)(2,1)S(1)} %pad_maximum_fusion.3), channel_id=1, source_target_pairs={{0,16},{8,24},{16,0},{24,8},{1,17},{9,25},{17,1},{25,9},{2,18},{10... | collective-permute-start | bytes 884744 | tf_op jit(solution)/shard_map/ppermute | solution.py:326
  37.9 0.0 copy-done.7
  37.9 0.0 collective-permute-done.11.swapped
  37.9 0.0 collective-permute-done.12.swapped_value
  37.9 0.0 collective-permute-done.7.weights_other
  37.9 0.0 copy-done.3
  38.0 4.7 %early.1 = (f32[4,400,128]{2,1,0:T(8,128)S(1)}, bf16[4,128,384]{2,1,0:T(8,128)(2,1)S(1)}, bf16[768,384]{1,0:T(8,128)(2,1)S(1)}, bf16[384,768]{1,0:T(8,128)(2,1)S(1)}) custom-call(bf16[4,160,768]{2,1,0:T(8,128)(2,1)S(1)} %pad_maximum_fusion.weights_mine, bf16[4,160,768]{2,1,0:T(8,128)(2,1)S(1)} %collective-permute-done.7.weights_other, ...), custom_call_target="tpu_custom_call" | custom-call | tf_op jit(solution)/shard_map/early/pallas_call | solution.py:415
  42.7 2.1 %collective-permute-done.13.block = bf16[4,64,768]{2,1,0:T(8,128)(2,1)S(1)} collective-permute-done((bf16[4,64,768]{2,1,0:T(8,128)(2,1)S(1)}, bf16[4,64,768]{2,1,0:T(8,128)(2,1)S(1)}, u32[]{:S(2)}, u32[]{:S(2)}) %collective-permute-start.13) | collective-permute-done | bytes 393248 | tf_op jit(solution)/shard_map/ppermute | solution.py:320
  44.8 1.8 %late.3 = (f32[1,400,128]{2,1,0:T(8,128)S(1)}, f32[1,400,128]{2,1,0:T(8,128)S(1)}) custom-call(f32[4,400,128]{2,1,0:T(8,128)S(1)} %get-tuple-element.43.partial, bf16[4,128,384]{2,1,0:T(8,128)(2,1)S(1)} %get-tuple-element.44.queries, bf16[768,384]{1,0:T(8,128)(2,1)S(1)} %get-tuple-element.45.key_weight, bf16[384,768]{1,0:T(8,128)(2,1)S(1)} %get-tuple-element.46.value_weight, ...), custom_call_target="tpu_custom_call" | custom-call | tf_op jit(solution)/shard_map/late/pallas_call | solution.py:435
  46.6 0.0 copy-start
  46.6 0.0 copy-start.2
  46.6 0.1 collective-permute-start.15
  46.7 1.8 %late.2 = (f32[1,400,128]{2,1,0:T(8,128)S(1)}, f32[1,400,128]{2,1,0:T(8,128)S(1)}) custom-call(f32[4,400,128]{2,1,0:T(8,128)S(1)} %get-tuple-element.43.partial, bf16[4,128,384]{2,1,0:T(8,128)(2,1)S(1)} %get-tuple-element.44.queries, bf16[768,384]{1,0:T(8,128)(2,1)S(1)} %get-tuple-element.45.key_weight, bf16[384,768]{1,0:T(8,128)(2,1)S(1)} %get-tuple-element.46.value_weight, ...), custom_call_target="tpu_custom_call" | custom-call | tf_op jit(solution)/shard_map/late/pallas_call | solution.py:435
  48.5 0.6 %collective-permute-start.14 = (f32[1,400,128]{2,1,0:T(8,128)S(1)}, f32[1,400,128]{2,1,0:T(8,128)S(1)}, u32[]{:S(2)}, u32[]{:S(2)}) collective-permute-start(f32[1,400,128]{2,1,0:T(8,128)S(1)} %get-tuple-element.49), channel_id=1, source_target_pairs={{0,1},{1,0},{2,3},{3,2},{4,5},{5,4},{6,7},{7,6},{8,9},{9,8},{10,11... | collective-permute-start | bytes 614408 | tf_op jit(solution)/shard_map/ppermute | solution.py:315
  49.0 0.0 collective-permute-done.6
  49.0 0.1 pad_maximum_fusion.2.weight_parts
  49.1 0.0 collective-permute-done.15.refs_3_
  49.1 1.0 %collective-permute-done.14.refs_2_ = f32[1,400,128]{2,1,0:T(8,128)S(1)} collective-permute-done((f32[1,400,128]{2,1,0:T(8,128)S(1)}, f32[1,400,128]{2,1,0:T(8,128)S(1)}, u32[]{:S(2)}, u32[]{:S(2)}) %collective-permute-start.14) | collective-permute-done | bytes 204832 | tf_op jit(solution)/shard_map/ppermute | solution.py:315
  50.1 0.0 copy-done
  50.1 0.0 copy-done.2
  50.1 1.2 %finish.1 = bf16[4,64,768]{2,1,0:T(8,128)(2,1)} custom-call(bf16[4,96,768]{2,1,0:T(8,128)(2,1)S(1)} %pad_maximum_fusion.2.weight_parts, bf16[4,64,768]{2,1,0:T(8,128)(2,1)S(1)} %copy-done, bf16[4,64,768]{2,1,0:T(8,128)(2,1)S(1)} %copy-done.2, f32[1,400,128]{2,1,0:T(8,128)S(1)} %get-tuple-element.47.refs_0_, f32[1,400,128]{2,1,0:T(8,128)S(1)} %get-tuple-element.48.refs_1_, ...), custom_call_target="tpu_custom_call" | custom-call | tf_op jit(solution)/shard_map/finish/pallas_call | solution.py:444
  (4 shorter events, 0.1 us)
Async XLA Ops:
  2.9 14.5 %copy-start.1 = (bf16[4,64,768]{2,1,0:T(8,128)(2,1)S(1)}, bf16[4,64,768]{2,1,0:T(8,128)(2,1)}, u32[]{:S(2)}) copy-start(bf16[4,64,768]{2,1,0:T(8,128)(2,1)} %get-tuple-element.37.shifted) | copy-start | bytes 1179652
  3.0 14.4 %copy-start.6 = (bf16[96,768]{1,0:T(8,128)(2,1)S(1)}, bf16[96,768]{1,0:T(8,128)(2,1)}, u32[]{:S(2)}) copy-start(bf16[96,768]{1,0:T(8,128)(2,1)} %get-tuple-element.33) | copy-start | bytes 442372
  3.0 14.4 %collective-permute-start = (bf16[4,64,768]{2,1,0:T(8,128)(2,1)}, bf16[4,64,768]{2,1,0:T(8,128)(2,1)S(1)}, u32[]{:S(2)}, u32[]{:S(2)}) collective-permute-start(bf16[4,64,768]{2,1,0:T(8,128)(2,1)} %get-tuple-element.28.refs_0_), channel_id=1, source_target_pairs={{0,2},{1,3},{2,4},{3,5},{4,6},{5,7},{6,0},{7,1},{8,10},{9,11},{10,... | collective-permute-start | bytes 1179656 | tf_op jit(solution)/shard_map/ppermute | solution.py:320
  6.0 9.4 %collective-permute-start.1 = (bf16[96,768]{1,0:T(8,128)(2,1)}, bf16[96,768]{1,0:T(8,128)(2,1)S(1)}, u32[]{:S(2)}, u32[]{:S(2)}) collective-permute-start(bf16[96,768]{1,0:T(8,128)(2,1)} %get-tuple-element.33), channel_id=1, source_target_pairs={{0,8},{8,0},{16,24},{24,16},{1,9},{9,1},{17,25},{25,17},{2,10},{10... | collective-permute-start | bytes 442376 | tf_op jit(solution)/shard_map/ppermute | solution.py:326
  7.5 8.5 %collective-permute-start.2 = (bf16[96,768]{1,0:T(8,128)(2,1)}, bf16[96,768]{1,0:T(8,128)(2,1)S(1)}, u32[]{:S(2)}, u32[]{:S(2)}) collective-permute-start(bf16[96,768]{1,0:T(8,128)(2,1)} %get-tuple-element.33), channel_id=1, source_target_pairs={{0,16},{8,24},{16,0},{24,8},{1,17},{9,25},{17,1},{25,9},{2,18},{10... | collective-permute-start | bytes 442376 | tf_op jit(solution)/shard_map/ppermute | solution.py:326
  9.1 7.0 %collective-permute-start.3 = (bf16[96,768]{1,0:T(8,128)(2,1)}, bf16[96,768]{1,0:T(8,128)(2,1)S(1)}, u32[]{:S(2)}, u32[]{:S(2)}) collective-permute-start(bf16[96,768]{1,0:T(8,128)(2,1)} %get-tuple-element.33), channel_id=1, source_target_pairs={{0,24},{8,16},{16,8},{24,0},{1,25},{9,17},{17,9},{25,1},{2,26},{10... | collective-permute-start | bytes 442376 | tf_op jit(solution)/shard_map/ppermute | solution.py:326
  9.5 21.4 %copy-start.5 = (bf16[96,768]{1,0:T(8,128)(2,1)S(1)}, bf16[96,768]{1,0:T(8,128)(2,1)}, u32[]{:S(2)}) copy-start(bf16[96,768]{1,0:T(8,128)(2,1)} %param.22) | copy-start | bytes 442372
  15.4 2.5 %copy-start.4 = (bf16[800,128]{1,0:T(8,128)(2,1)S(1)}, bf16[800,128]{1,0:T(8,128)(2,1)}, u32[]{:S(2)}) copy-start(bf16[800,128]{1,0:T(8,128)(2,1)} %bias.1) | copy-start | bytes 614404
  17.5 20.5 %copy-start.7 = (bf16[384]{0:T(512)(128)(2,1)S(1)}, bf16[384]{0:T(512)(128)(2,1)}, u32[]{:S(2)}) copy-start(bf16[384]{0:T(512)(128)(2,1)} %param.19) | copy-start | bytes 2308
  17.5 20.5 %copy-start.3 = (bf16[4,64,768]{2,1,0:T(8,128)(2,1)S(1)}, bf16[4,64,768]{2,1,0:T(8,128)(2,1)}, u32[]{:S(2)}) copy-start(bf16[4,64,768]{2,1,0:T(8,128)(2,1)} %get-tuple-element.28.refs_0_) | copy-start | bytes 1179652
  17.5 20.5 %collective-permute-start.7 = (bf16[4,160,768]{2,1,0:T(8,128)(2,1)S(1)}, bf16[4,160,768]{2,1,0:T(8,128)(2,1)S(1)}, u32[]{:S(2)}, u32[]{:S(2)}) collective-permute-start(bf16[4,160,768]{2,1,0:T(8,128)(2,1)S(1)} %pad_maximum_fusion.weights_mine), channel_id=1, source_target_pairs={{0,1},{1,0},{2,3},{3,2},{4,5},{5,4},{6,7},{7,6},{8,9},{9,8},{10,11... | collective-permute-start | bytes 2949128 | tf_op jit(solution)/shard_map/ppermute | solution.py:315
  17.6 13.3 %collective-permute-start.4 = (bf16[4,64,768]{2,1,0:T(8,128)(2,1)S(1)}, bf16[4,64,768]{2,1,0:T(8,128)(2,1)S(1)}, u32[]{:S(2)}, u32[]{:S(2)}) collective-permute-start(bf16[4,64,768]{2,1,0:T(8,128)(2,1)S(1)} %collective-permute-done.refs_1_), channel_id=1, source_target_pairs={{0,2},{1,3},{2,4},{3,5},{4,6},{5,7},{6,0},{7,1},{8,10},{9,11},{10,... | collective-permute-start | bytes 1179656 | tf_op jit(solution)/shard_map/ppermute | solution.py:320
  17.9 14.5 %collective-permute-start.10 = (bf16[800,128]{1,0:T(8,128)(2,1)S(1)}, bf16[800,128]{1,0:T(8,128)(2,1)S(1)}, u32[]{:S(2)}, u32[]{:S(2)}) collective-permute-start(bf16[800,128]{1,0:T(8,128)(2,1)S(1)} %copy-done.4), channel_id=1, source_target_pairs={{0,24},{8,16},{16,8},{24,0},{1,25},{9,17},{17,9},{25,1},{2,26},{10... | collective-permute-start | bytes 614408 | tf_op jit(solution)/shard_map/ppermute | solution.py:326
  20.2 12.2 %collective-permute-start.8 = (bf16[800,128]{1,0:T(8,128)(2,1)S(1)}, bf16[800,128]{1,0:T(8,128)(2,1)S(1)}, u32[]{:S(2)}, u32[]{:S(2)}) collective-permute-start(bf16[800,128]{1,0:T(8,128)(2,1)S(1)} %copy-done.4), channel_id=1, source_target_pairs={{0,8},{8,0},{16,24},{24,16},{1,9},{9,1},{17,25},{25,17},{2,10},{10... | collective-permute-start | bytes 614408 | tf_op jit(solution)/shard_map/ppermute | solution.py:326
  20.7 11.6 %collective-permute-start.9 = (bf16[800,128]{1,0:T(8,128)(2,1)S(1)}, bf16[800,128]{1,0:T(8,128)(2,1)S(1)}, u32[]{:S(2)}, u32[]{:S(2)}) collective-permute-start(bf16[800,128]{1,0:T(8,128)(2,1)S(1)} %copy-done.4), channel_id=1, source_target_pairs={{0,16},{8,24},{16,0},{24,8},{1,17},{9,25},{17,1},{25,9},{2,18},{10... | collective-permute-start | bytes 614408 | tf_op jit(solution)/shard_map/ppermute | solution.py:326
  30.9 5.4 %collective-permute-start.5 = (bf16[1,96,768]{2,1,0:T(8,128)(2,1)S(1)}, bf16[1,96,768]{2,1,0:T(8,128)(2,1)S(1)}, u32[]{:S(2)}, u32[]{:S(2)}) collective-permute-start(bf16[1,96,768]{2,1,0:T(8,128)(2,1)S(1)} %bitcast.11), channel_id=1, source_target_pairs={{0,8},{8,0},{16,24},{24,16},{1,9},{9,1},{17,25},{25,17},{2,10},{10... | collective-permute-start | bytes 442376 | tf_op jit(solution)/shard_map/ppermute | solution.py:326
  32.4 12.4 %collective-permute-start.13 = (bf16[4,64,768]{2,1,0:T(8,128)(2,1)S(1)}, bf16[4,64,768]{2,1,0:T(8,128)(2,1)S(1)}, u32[]{:S(2)}, u32[]{:S(2)}) collective-permute-start(bf16[4,64,768]{2,1,0:T(8,128)(2,1)S(1)} %collective-permute-done.4.refs_2_), channel_id=1, source_target_pairs={{0,2},{1,3},{2,4},{3,5},{4,6},{5,7},{6,0},{7,1},{8,10},{9,11},{10,... | collective-permute-start | bytes 1179656 | tf_op jit(solution)/shard_map/ppermute | solution.py:320
  32.8 5.1 %collective-permute-start.12 = (bf16[4,288,128]{2,1,0:T(8,128)(2,1)S(1)}, bf16[4,288,128]{2,1,0:T(8,128)(2,1)S(1)}, u32[]{:S(2)}, u32[]{:S(2)}) collective-permute-start(bf16[4,288,128]{2,1,0:T(8,128)(2,1)S(1)} %slice.12), channel_id=1, source_target_pairs={{0,1},{1,0},{2,3},{3,2},{4,5},{5,4},{6,7},{7,6},{8,9},{9,8},{10,11... | collective-permute-start | bytes 884744 | tf_op jit(solution)/shard_map/ppermute | solution.py:315
  32.9 5.0 %collective-permute-start.11 = (bf16[4,256,128]{2,1,0:T(8,128)(2,1)S(1)}, bf16[4,256,128]{2,1,0:T(8,128)(2,1)S(1)}, u32[]{:S(2)}, u32[]{:S(2)}) collective-permute-start(bf16[4,256,128]{2,1,0:T(8,128)(2,1)S(1)} %slice.11), channel_id=1, source_target_pairs={{0,1},{1,0},{2,3},{3,2},{4,5},{5,4},{6,7},{7,6},{8,9},{9,8},{10,11... | collective-permute-start | bytes 786440 | tf_op jit(solution)/shard_map/ppermute | solution.py:315
  36.3 12.7 %collective-permute-start.6 = (bf16[2,96,768]{2,1,0:T(8,128)(2,1)S(1)}, bf16[2,96,768]{2,1,0:T(8,128)(2,1)S(1)}, u32[]{:S(2)}, u32[]{:S(2)}) collective-permute-start(bf16[2,96,768]{2,1,0:T(8,128)(2,1)S(1)} %pad_maximum_fusion.3), channel_id=1, source_target_pairs={{0,16},{8,24},{16,0},{24,8},{1,17},{9,25},{17,1},{25,9},{2,18},{10... | collective-permute-start | bytes 884744 | tf_op jit(solution)/shard_map/ppermute | solution.py:326
  46.6 3.5 %copy-start = (bf16[4,64,768]{2,1,0:T(8,128)(2,1)S(1)}, bf16[4,64,768]{2,1,0:T(8,128)(2,1)}, u32[]{:S(2)}) copy-start(bf16[4,64,768]{2,1,0:T(8,128)(2,1)} %activations.1) | copy-start | bytes 1179652
  46.6 3.5 %copy-start.2 = (bf16[4,64,768]{2,1,0:T(8,128)(2,1)S(1)}, bf16[4,64,768]{2,1,0:T(8,128)(2,1)}, u32[]{:S(2)}) copy-start(bf16[4,64,768]{2,1,0:T(8,128)(2,1)} %output_gate.1) | copy-start | bytes 1179652
  46.6 2.5 %collective-permute-start.15 = (f32[1,400,128]{2,1,0:T(8,128)S(1)}, f32[1,400,128]{2,1,0:T(8,128)S(1)}, u32[]{:S(2)}, u32[]{:S(2)}) collective-permute-start(f32[1,400,128]{2,1,0:T(8,128)S(1)} %get-tuple-element.50), channel_id=1, source_target_pairs={{0,1},{1,0},{2,3},{3,2},{4,5},{5,4},{6,7},{7,6},{8,9},{9,8},{10,11... | collective-permute-start | bytes 614408 | tf_op jit(solution)/shard_map/ppermute | solution.py:315
  48.5 1.6 %collective-permute-start.14 = (f32[1,400,128]{2,1,0:T(8,128)S(1)}, f32[1,400,128]{2,1,0:T(8,128)S(1)}, u32[]{:S(2)}, u32[]{:S(2)}) collective-permute-start(f32[1,400,128]{2,1,0:T(8,128)S(1)} %get-tuple-element.49), channel_id=1, source_target_pairs={{0,1},{1,0},{2,3},{3,2},{4,5},{5,4},{6,7},{7,6},{8,9},{9,8},{10,11... | collective-permute-start | bytes 614408 | tf_op jit(solution)/shard_map/ppermute | solution.py:315
